TPU v7x, 128 devices: a whole 4x4x4 slice. The times are simulated.
128 devices in a mesh: dp: 32 (over z, y, core), tensor: 4 (over x).
Axes of the slice: x: 4, y: 4, z: 4, core: 2. Of those that a mesh axis runs over, the one named last changes fastest.
Arguments:
- hidden_in: bfloat16 [32768, 640], P(('dp', 'tensor')), may hold values from -6 to 6
- out_grad: bfloat16 [32768, 640], P(('dp', 'tensor')), may hold values from -6 to 6
- segment_ids: int32 [32768], P('dp'), may hold values from -1 to 1023, as said below
- gain_input: bfloat16 [640], P('dp'), may hold values from 0.25 to 1.75
- w_query: bfloat16 [640, 4, 256], P('dp', 'tensor'), may hold values from -0.25 to 0.25
- w_key: bfloat16 [640, 256], P('dp'), may hold values from -0.25 to 0.25
- w_value: bfloat16 [640, 256], P('dp'), may hold values from -0.25 to 0.25
- gain_query: bfloat16 [256], P('dp'), may hold values from 0.25 to 1.75
- gain_key: bfloat16 [256], P('dp'), may hold values from 0.25 to 1.75
- w_out: bfloat16 [640, 4, 256], P('dp', 'tensor'), may hold values from -0.1875 to 0.1875
- gain_attn: bfloat16 [640], P('dp'), may hold values from 0.25 to 1.75
- gain_ffin: bfloat16 [640], P('dp'), may hold values from 0.25 to 1.75
- w_gate: bfloat16 [640, 2048], P('dp', 'tensor'), may hold values from -0.25 to 0.25
- w_up: bfloat16 [640, 2048], P('dp', 'tensor'), may hold values from -0.25 to 0.25
- w_down: bfloat16 [640, 2048], P('dp', 'tensor'), may hold values from -0.125 to 0.125
- gain_ffout: bfloat16 [640], P('dp'), may hold values from 0.25 to 1.75
Outputs:
- layer_out: bfloat16 [32768, 640], P(('dp', 'tensor'))
- input_grad: float32 [32768, 640], P(('dp', 'tensor'))
- grad_gain_input: float32 [640], P('dp')
- grad_w_query: float32 [640, 4, 256], P('dp', 'tensor')
- grad_w_key: float32 [640, 256], P('dp')
- grad_w_value: float32 [640, 256], P('dp')
- grad_gain_query: float32 [256], P('dp')
- grad_gain_key: float32 [256], P('dp')
- grad_w_out: float32 [640, 4, 256], P('dp', 'tensor')
- grad_gain_attn: float32 [640], P('dp')
- grad_gain_ffin: float32 [640], P('dp')
- grad_w_gate: float32 [640, 2048], P('dp', 'tensor')
- grad_w_up: float32 [640, 2048], P('dp', 'tensor')
- grad_w_down: float32 [640, 2048], P('dp', 'tensor')
- grad_gain_ffout: float32 [640], P('dp')
Inputs may be any that keep to these rules, and one draw needn't show every extreme that they name: `segment_ids`: each block of 1024 ids, in order, is one packed row: a live row's id is the index, within its block, of the first row of its document, so ids never fall over the live rows; a document is a run of equal ids of at most 1024 rows, and the live rows are followed by a tail of fewer than 256 entries of -1.
All inputs are finite; a program needn't handle non-finite values.
Results may differ from a plain program's by a relative error of at most 0.033.
Values may be sent and summed in bfloat16 or wider, within the bound.
No kernel may reach another device: no remote copies, remote signals or barrier semaphores. Data moves between devices by JAX's collectives and lax.ppermute only.
A program may use at most 128 MiB of HBM per device.

v0:
```python
import jax
import jax.numpy as jnp
from jax import lax
from jax.experimental import pallas as pl
from jax.experimental.pallas import tpu as pltpu
from jax.sharding import Mesh, PartitionSpec as P

WINDOW = 512
EPS = 1e-06
ROPE_BASE = 10000.0
NEGATIVE = -1e30
ZS, YS, CS, XS = 4, 4, 2, 4
CHIP = ("z", "y", "x")
EVERY = ("z", "y", "core", "x")
DPS = 32
OWN = 20
PAD = 24
DM = 640
DP = DPS * PAD
ROWS = 256
KEYS = 3 * ROWS
HQ = 4
HD = 256
HALF = HD // 2
ATT = 768
FFC = 1536
SCALE = HD**-0.5
GELU_C = 0.7978845608028654
GELU_A = 0.044715
BF = jnp.bfloat16
F32 = jnp.float32


def norm_of(values_in, width):
    inverse = lax.rsqrt(
        jnp.sum(values_in * values_in, axis=-1, keepdims=True) * (1.0 / width) + EPS
    )
    return values_in * inverse, inverse


def norm_back(normed, inverse, upstream, width):
    mean = jnp.sum(upstream * normed, axis=-1, keepdims=True) * (1.0 / width)
    return inverse * (upstream - normed * mean)


def rotate(values_in, cosine, sine):
    first, second = values_in[:, :HALF], values_in[:, HALF:]
    return jnp.concatenate(
        [first * cosine - second * sine, second * cosine + first * sine], axis=1
    )


def dot(lhs, rhs, lhs_dim, rhs_dim):
    return lax.dot_general(
        lhs, rhs, (((lhs_dim,), (rhs_dim,)), ((), ())), preferred_element_type=F32
    )


def spread_matrix():
    row = lax.broadcasted_iota(jnp.int32, (DM, DP), 0)
    col = lax.broadcasted_iota(jnp.int32, (DM, DP), 1)
    return ((col % PAD < OWN) & (row == (col // PAD) * OWN + col % PAD)).astype(BF)


def head_matrix(step):
    row = lax.broadcasted_iota(jnp.int32, (DPS * step, HD), 0)
    col = lax.broadcasted_iota(jnp.int32, (DPS * step, HD), 1)
    return ((row // step == col // 8) & (row % step == col % 8)).astype(BF)


def fetch(gathered, held, sems, first, size):
    copies = [
        pltpu.make_async_copy(gathered.at[:, x, :, first : first + size], held.at[x], sems.at[x])
        for x in range(XS)
    ]
    for copy in copies:
        copy.start()
    return copies


def cut(held, x, first, size):
    return held[x, :, :, first : first + size].reshape(DP, size)


def kv_weights(watt):
    return jnp.concatenate([cut(watt, x, 512, 128) for x in range(XS)], axis=1)


def pack_kernel(wqo_ref, wg_ref, wu_ref, wd_ref, wk_ref, wv_ref, gains_ref, at_ref, out):
    out[...] = jnp.zeros(out.shape, BF)
    out[0:OWN, 0:512] = wqo_ref[...]
    at = at_ref[0]
    kv = jnp.where(
        jnp.broadcast_to(at, (OWN, 256)) < 2, wk_ref[...].astype(F32), wv_ref[...].astype(F32)
    )
    kv = jnp.where(jnp.broadcast_to(at % 2, (OWN, 128)) == 0, kv[:, :128], kv[:, 128:])
    out[0:OWN, 512:640] = kv.astype(BF)
    out[:, 640:768] = gains_ref[...].T[:PAD].astype(BF)
    out[0:OWN, 768:1280] = wg_ref[...]
    out[0:OWN, 1280:1792] = wu_ref[...]
    out[0:OWN, 1792:2304] = wd_ref[...]


def forward_kernel(
    core_ref, gathered, normed_ref, cosine_ref, sine_ref, bias_ref, heads_ref, resid_ref, up_ref,
    spread_ref,
    gains_out, rows_out, qraw_out, kvraw_out, q_out, k_out, v_out, probs_out, mixed_out,
    layer_out, dres_out, dattn_out, away_out, sums_out, z_s, dg_s, du_s, rows_t_out, ff_t_out,
    attn_t_out, gate_s, upp_s, watt, sems, wff, ff_sems,
):
    attend_copies = fetch(gathered, watt, sems, 0, ATT)
    copies = fetch(gathered, wff, ff_sems, ATT, FFC)
    for copy in attend_copies:
        copy.wait()
    gains = cut(watt, 0, 640, 128).astype(F32).T
    gains_out[0:8] = gains[0:8]
    head_gains = dot(gains.astype(BF), heads_ref[...], 1, 0)
    gains_out[8:16] = jnp.concatenate([head_gains[0:8]] * 3, axis=1)
    query_gains, key_gains = head_gains[4:5], head_gains[5:6]
    rows = (normed_ref[...] * gains[0:1]).astype(BF)
    rows_out[...] = rows
    kv_raw = dot(rows, kv_weights(watt), 1, 0)
    kvraw_out[...] = kv_raw
    key_norm, _ = norm_of(kv_raw[:, :HD], HD)
    key = rotate(key_norm * key_gains, cosine_ref[...], sine_ref[...]).astype(BF)
    value = kv_raw[:, HD:].astype(BF)
    k_out[...] = key
    v_out[...] = value
    rows_own = rows[2 * ROWS :]
    cosine, sine = cosine_ref[2 * ROWS :], sine_ref[2 * ROWS :]
    attn = jnp.zeros((ROWS, DP), F32)
    for head in range(HQ):
        at = slice(head * HD, (head + 1) * HD)
        query_raw = dot(rows_own, cut(watt, head, 0, 256), 1, 0)
        qraw_out[:, at] = query_raw
        query_norm, _ = norm_of(query_raw, HD)
        query = rotate(query_norm * query_gains, cosine, sine).astype(BF)
        q_out[:, at] = query
        scores = dot(query, key, 1, 1) * SCALE + bias_ref[...]
        exponent = jnp.exp(scores - jnp.max(scores, axis=-1, keepdims=True))
        probs = exponent * (1.0 / jnp.sum(exponent, axis=-1, keepdims=True))
        probs = probs.astype(BF)
        probs_out[head] = probs
        mixed = dot(probs, value, 1, 0).astype(BF)
        mixed_out[:, at] = mixed
        attn = attn + dot(mixed, cut(watt, head, 256, 256), 1, 1)
    attn_gains, ffin_gains, ffout_gains = gains[1:2], gains[2:3], gains[3:4]
    spread = spread_ref[...]
    upstream = up_ref[...]
    attn_normed, attn_inv = norm_of(attn, DM)
    mid = resid_ref[...] + attn_normed * attn_gains
    mid_normed, mid_inv = norm_of(mid, DM)
    rows = (mid_normed * ffin_gains).astype(BF)
    ff_sum = jnp.zeros((ROWS, DP), F32)
    for x in range(XS):
        at = slice(x * 512, (x + 1) * 512)
        copies[x].wait()
        gate = dot(rows, cut(wff, x, 0, 512), 1, 0)
        up = dot(rows, cut(wff, x, 512, 512), 1, 0)
        gate_s[:, at] = gate
        upp_s[:, at] = up
        act = 0.5 * gate * (1.0 + jnp.tanh(GELU_C * (gate + GELU_A * gate * gate * gate)))
        hidden = (act * up).astype(BF)
        z_s[:, at] = hidden
        ff_sum = ff_sum + dot(hidden, cut(wff, x, 1024, 512), 1, 1)
    ff_normed, ff_inv = norm_of(ff_sum, DM)
    layer = (mid + ff_normed * ffout_gains).astype(BF)
    layer_out[...] = dot(layer, spread, 1, 1).astype(BF)
    grad_gout = jnp.sum(upstream * ff_normed, axis=0, keepdims=True)
    grad_ff = norm_back(ff_normed, ff_inv, upstream * ffout_gains, DM).astype(BF)
    grad_mid = jnp.zeros((ROWS, DP), F32)
    for x in range(XS):
        at = slice(x * 512, (x + 1) * 512)
        grad_hidden = dot(grad_ff, cut(wff, x, 1024, 512), 1, 0)
        gate, up = gate_s[:, at], upp_s[:, at]
        curve = jnp.tanh(GELU_C * (gate + GELU_A * gate * gate * gate))
        slope = 0.5 * (1.0 + curve) + 0.5 * gate * (1.0 - curve * curve) * (
            GELU_C * (1.0 + 3.0 * GELU_A * gate * gate)
        )
        grad_gate = (grad_hidden * up * slope).astype(BF)
        grad_up = (grad_hidden * (0.5 * gate * (1.0 + curve))).astype(BF)
        dg_s[:, at] = grad_gate
        du_s[:, at] = grad_up
        grad_mid = grad_mid + dot(grad_gate, cut(wff, x, 0, 512), 1, 1)
        grad_mid = grad_mid + dot(grad_up, cut(wff, x, 512, 512), 1, 1)
    grad_gfin = jnp.sum(grad_mid * mid_normed, axis=0, keepdims=True)
    grad_resid = upstream + norm_back(mid_normed, mid_inv, grad_mid * ffin_gains, DM)
    dres_out[...] = grad_resid
    grad_gattn = jnp.sum(grad_resid * attn_normed, axis=0, keepdims=True)
    dattn_out[...] = norm_back(attn_normed, attn_inv, grad_resid * attn_gains, DM).astype(BF)
    zero = jnp.zeros((1, DP), F32)
    sums_out[...] = jnp.concatenate(
        [zero, grad_gattn, grad_gfin, grad_gout, zero, zero, zero, zero], axis=0
    )
    rows_t = dot(spread, rows, 1, 1).astype(BF)
    ff_t = dot(spread, grad_ff, 1, 1).astype(BF)
    attn_t = dot(spread, dattn_out[...], 1, 1).astype(BF)
    rows_t_out[...] = rows_t
    ff_t_out[...] = ff_t
    attn_t_out[...] = attn_t
    feed_half(1 - core_ref[0], away_out, rows_t, ff_t, attn_t, z_s, dg_s, du_s, mixed_out)


def feed_half(half, out, rows_t, ff_t, attn_t, z_ref, dg_ref, du_ref, mixed_ref):
    for x in range(XS):
        cols = pl.ds(pl.multiple_of(x * 512 + half * 256, 256), 256)
        for part, (lhs, rhs) in enumerate(((rows_t, dg_ref), (rows_t, du_ref), (ff_t, z_ref))):
            grad = dot(lhs, rhs[:, cols], 1, 0).astype(BF)
            out[x, :, part * 256 : (part + 1) * 256] = grad
        cols = pl.ds(pl.multiple_of(x * 256 + half * 128, 128), 128)
        out[x, :, 768:896] = dot(attn_t, mixed_ref[:, cols], 1, 0).astype(BF)


def feed_keep_kernel(
    core_ref, z_ref, dg_ref, du_ref, rows_t_ref, ff_t_ref, attn_t_ref, mixed_ref, keep_out
):
    feed_half(
        core_ref[0], keep_out, rows_t_ref[...], ff_t_ref[...], attn_t_ref[...],
        z_ref, dg_ref, du_ref, mixed_ref,
    )


def attend_back_kernel(
    core_ref, gathered, dattn_ref, rows_ref, normed_ref, qraw_ref, kvraw_ref, q_ref, k_ref, v_ref,
    probs_ref, cosine_ref, sine_ref, gains_ref, sums_ref, spread_ref, heads_ref,
    keep_out, away_out, dkv_out, part_out, wq_s, wkv_s, watt, sems,
):
    copies = fetch(gathered, watt, sems, 0, ATT)
    spread = spread_ref[...]
    query_gains, key_gains = gains_ref[12:13, :HD], gains_ref[13:14, :HD]
    grad_attn = dattn_ref[...]
    rows_t = dot(spread, rows_ref[...], 1, 1).astype(BF)
    rows_own_t = rows_t[:, 2 * ROWS :]
    key, value = k_ref[...], v_ref[...]
    cosine, sine = cosine_ref[2 * ROWS :], sine_ref[2 * ROWS :]
    for copy in copies:
        copy.wait()
    grad_key = jnp.zeros((KEYS, HD), F32)
    grad_value = jnp.zeros((KEYS, HD), F32)
    part = jnp.zeros((ROWS, DP), F32)
    grad_gq = jnp.zeros((1, HD), F32)
    for head in range(HQ):
        at = slice(head * HD, (head + 1) * HD)
        grad_mixed = dot(grad_attn, cut(watt, head, 256, 256), 1, 0).astype(BF)
        probs_low = probs_ref[head]
        probs = probs_low.astype(F32)
        grad_value = grad_value + dot(probs_low, grad_mixed, 0, 0)
        grad_probs = dot(grad_mixed, value, 1, 1)
        grad_scores = (
            probs * (grad_probs - jnp.sum(probs * grad_probs, axis=-1, keepdims=True))
        ).astype(BF)
        grad_query = dot(grad_scores, key, 1, 0) * SCALE
        grad_key = grad_key + dot(grad_scores, q_ref[:, at], 0, 0)
        query_norm, query_inv = norm_of(qraw_ref[:, at], HD)
        grad_query = rotate(grad_query, cosine, -sine)
        grad_gq = grad_gq + jnp.sum(grad_query * query_norm, axis=0, keepdims=True)
        grad_raw = norm_back(query_norm, query_inv, grad_query * query_gains, HD).astype(BF)
        part = part + dot(grad_raw, cut(watt, head, 0, 256), 1, 1)
        wq_s[:, at] = dot(rows_own_t, grad_raw, 1, 0).astype(BF)
    part_out[...] = part
    key_norm, key_inv = norm_of(kvraw_ref[:, :HD], HD)
    grad_key = rotate(grad_key * SCALE, cosine_ref[...], -sine_ref[...])
    grad_gk = jnp.sum(grad_key * key_norm, axis=0, keepdims=True)
    grad_key = norm_back(key_norm, key_inv, grad_key * key_gains, HD)
    grad_kv = jnp.concatenate([grad_key, grad_value], axis=1).astype(BF)
    dkv_out[...] = grad_kv
    wkv_s[...] = dot(rows_t, grad_kv, 1, 0).astype(BF)
    kv_part = dot(grad_kv, kv_weights(watt), 1, 1)
    grad_gin = jnp.sum(kv_part * normed_ref[...], axis=0, keepdims=True)
    grad_gin = grad_gin + jnp.sum(part * normed_ref[2 * ROWS :], axis=0, keepdims=True)
    model = jnp.concatenate([grad_gin, sums_ref[1:8], jnp.zeros((120, DP), F32)], axis=0)
    zeros = jnp.zeros((1, HD), F32)
    heads = jnp.concatenate(
        [zeros, zeros, zeros, zeros, grad_gq, grad_gk, zeros, zeros, jnp.zeros((120, HD), F32)],
        axis=0,
    )
    gains = dot(spread, model.astype(BF), 1, 1) + dot(heads_ref[...], heads.astype(BF), 1, 1)
    gains = gains.astype(BF)
    core = core_ref[0]
    own_kv = jnp.broadcast_to(core, (DM, 128)) == 0
    for x in range(XS):
        for out, half in ((keep_out, core), (away_out, 1 - core)):
            cols = pl.ds(pl.multiple_of(x * 256 + half * 128, 128), 128)
            out[:, x, :, 0:128] = wq_s[:, cols].astype(F32).reshape(16, 40, 128).astype(BF)
        kv = wkv_s[:, x * 128 : (x + 1) * 128].astype(F32)
        kept = jnp.where(own_kv, kv, gains.astype(F32)).reshape(16, 40, 128).astype(BF)
        sent = jnp.where(own_kv, gains.astype(F32), kv).reshape(16, 40, 128).astype(BF)
        keep_out[:, x, :, 128:256] = kept
        away_out[:, x, :, 128:256] = sent


def call(kernel, outs, args, scratch=(), word=None, weights=None, flops=0, vmem=0):
    whole = pl.BlockSpec(memory_space=pltpu.VMEM)
    first, first_specs = [], []
    if word is not None:
        first, first_specs = [word], [pl.BlockSpec(memory_space=pltpu.SMEM)]
    shapes = [pltpu.VMEM(shape, kind) for shape, kind in scratch]
    if weights is not None:
        gathered, *sizes = weights
        first, first_specs = first + [gathered], first_specs + [pl.BlockSpec(memory_space=pl.ANY)]
        for size in sizes:
            shapes += [pltpu.VMEM((XS, DPS, PAD, size), BF), pltpu.SemaphoreType.DMA((XS,))]
    return pl.pallas_call(
        kernel,
        out_shape=[jax.ShapeDtypeStruct(shape, kind) for shape, kind in outs],
        in_specs=first_specs + [whole] * len(args),
        out_specs=[whole] * len(outs),
        scratch_shapes=shapes,
        compiler_params=pltpu.CompilerParams(vmem_limit_bytes=vmem * 2**20),
        cost_estimate=pl.CostEstimate(flops=flops, bytes_accessed=20 * 2**20, transcendentals=0),
    )(*first, *args)


def per_device(
    hidden_in,
    out_grad,
    segment_ids,
    gain_input,
    w_query,
    w_key,
    w_value,
    gain_query,
    gain_key,
    w_out,
    gain_attn,
    gain_ffin,
    w_gate,
    w_up,
    w_down,
    gain_ffout,
):
    at = lax.axis_index("x")
    core = lax.axis_index("core")

    gains_own = jnp.zeros((128, 128), F32)
    for row, gain in enumerate(
        (gain_input, gain_attn, gain_ffin, gain_ffout, gain_query, gain_key)
    ):
        size = gain.shape[0]
        gains_own = gains_own + jnp.pad(
            gain.astype(F32)[None], ((row, 127 - row), (0, 128 - size))
        )
    width = ATT + FFC
    at_word = at.astype(jnp.int32).reshape(1)
    whole = pl.BlockSpec(memory_space=pltpu.VMEM)
    packed = pl.pallas_call(
        pack_kernel,
        out_shape=jax.ShapeDtypeStruct((PAD, width), BF),
        in_specs=[whole] * 7 + [pl.BlockSpec(memory_space=pltpu.SMEM)],
        out_specs=whole,
    )(jnp.concatenate([w_query[:, 0], w_out[:, 0]], axis=1), w_gate, w_up, w_down, w_key, w_value, gains_own, at_word)
    gathered = lax.all_gather(packed, EVERY, axis=0, tiled=False).reshape(DPS, XS, PAD, width)

    before_one = lax.ppermute(hidden_in, "x", [(i, i + 1) for i in range(XS - 1)])
    before_two = lax.ppermute(hidden_in, "x", [(i, i + 2) for i in range(XS - 2)])
    rows_low = jnp.concatenate([before_two, before_one, hidden_in], axis=0)
    spread = spread_matrix()
    resid_all = dot(rows_low, spread, 1, 0)
    upstream = dot(out_grad, spread, 1, 0)
    normed_all, inverse_all = norm_of(resid_all, DM)
    resid_in = resid_all[2 * ROWS :]

    offsets = jnp.arange(segment_ids.shape[0], dtype=jnp.int32)
    live = segment_ids >= 0
    tail_start = jnp.sum(live.astype(jnp.int32))
    positions = offsets - jnp.where(live, segment_ids, tail_start)
    positions = jnp.concatenate([jnp.zeros((2 * ROWS,), jnp.int32), positions], axis=0)
    positions = lax.dynamic_slice_in_dim(positions, at * ROWS, KEYS, 0)
    frequency = ROPE_BASE ** (-2.0 * jnp.arange(HALF, dtype=F32) / HD)
    angles = positions.astype(F32)[:, None] * frequency[None, :]
    cosine, sine = jnp.cos(angles), jnp.sin(angles)
    ids = jnp.concatenate([jnp.full((2 * ROWS,), -2, jnp.int32), segment_ids], axis=0)
    key_ids = lax.dynamic_slice_in_dim(ids, at * ROWS, KEYS, 0)
    query_ids = key_ids[2 * ROWS :]
    row_at = lax.broadcasted_iota(jnp.int32, (ROWS, KEYS), 0)
    col_at = lax.broadcasted_iota(jnp.int32, (ROWS, KEYS), 1)
    gap = row_at + 2 * ROWS - col_at
    visible = (
        (query_ids[:, None] == key_ids[None, :])
        & (gap >= 0)
        & (gap < WINDOW)
        & ((query_ids[:, None] >= 0) | (gap == 0))
    )
    bias = jnp.where(visible, 0.0, NEGATIVE).astype(F32)

    core_word = core.astype(jnp.int32).reshape(1)
    (
        gains, rows_all, query_raw, kv_raw, query, key, value, probs, mixed,
        layer_out, grad_resid, grad_attn, away_ff, sums, *feed,
    ) = call(
        forward_kernel,
        [
            ((16, DP), F32),
            ((KEYS, DP), BF),
            ((ROWS, HQ * HD), F32),
            ((KEYS, 2 * HD), F32),
            ((ROWS, HQ * HD), BF),
            ((KEYS, HD), BF),
            ((KEYS, HD), BF),
            ((HQ, ROWS, KEYS), BF),
            ((ROWS, HQ * HD), BF),
            ((ROWS, DM), BF),
            ((ROWS, DP), F32),
            ((ROWS, DP), BF),
            ((XS, DM, 896), BF),
            ((8, DP), F32),
            ((ROWS, 2048), BF),
            ((ROWS, 2048), BF),
            ((ROWS, 2048), BF),
            ((DM, ROWS), BF),
            ((DM, ROWS), BF),
            ((DM, ROWS), BF),
        ],
        [normed_all, cosine, sine, bias, head_matrix(PAD), resid_in, upstream, spread],
        [((ROWS, 2048), F32), ((ROWS, 2048), F32)],
        word=core_word,
        weights=(gathered, ATT, FFC),
        flops=10**10,
        vmem=46,
    )
    swap = [(0, 1), (1, 0)]
    arrived_ff = lax.ppermute(away_ff, "core", swap)
    (keep_ff,) = call(
        feed_keep_kernel, [((XS, DM, 896), BF)], feed + [mixed], word=core_word, flops=2 * 10**9, vmem=20
    )
    both_ff = (keep_ff.astype(F32) + arrived_ff.astype(F32)).astype(BF)
    both_ff, grad_attn = lax.optimization_barrier((both_ff, grad_attn))
    column_ff = lax.psum_scatter(
        both_ff.reshape(XS * DM, 896), "x", scatter_dimension=0, tiled=True
    )
    keep_att, away_att, grad_kv, query_part = call(
        attend_back_kernel,
        [
            ((16, XS, 40, 256), BF),
            ((16, XS, 40, 256), BF),
            ((KEYS, 2 * HD), BF),
            ((ROWS, DP), F32),
        ],
        [
            grad_attn, rows_all, normed_all, query_raw, kv_raw, query, key, value, probs,
            cosine, sine, gains, sums, spread, head_matrix(OWN),
        ],
        [((DM, 1024), BF), ((DM, 512), BF)],
        word=core_word,
        weights=(gathered, ATT),
        flops=4 * 10**9,
        vmem=60,
    )
    arrived_att = lax.ppermute(away_att, "core", swap)
    from_one = lax.ppermute(
        grad_kv[ROWS : 2 * ROWS], "x", [(i + 1, i) for i in range(XS - 1)]
    )
    from_two = lax.ppermute(grad_kv[:ROWS], "x", [(i + 2, i) for i in range(XS - 2)])
    both_att = (keep_att.astype(F32) + arrived_att.astype(F32)).astype(BF)
    parts_att = lax.all_to_all(both_att.reshape(16, 160, 256), ("z", "y"), 0, 0, tiled=True)
    parts_att, column_ff = lax.optimization_barrier((parts_att, column_ff))
    row_att = jnp.sum(parts_att.astype(F32), axis=0).astype(BF)
    total_att = lax.psum_scatter(row_att, "x", scatter_dimension=0, tiled=True).astype(F32)
    parts_ff = lax.all_to_all(column_ff.reshape(16, 40, 896), ("z", "y"), 0, 0, tiled=True)
    total_ff = jnp.sum(parts_ff.astype(F32), axis=0)
    total = jnp.concatenate([total_ff, total_att], axis=1)

    grad_kv_own = (
        grad_kv[2 * ROWS :].astype(F32) + from_one.astype(F32) + from_two.astype(F32)
    ).astype(BF)
    kv_cols = gathered[:, :, :, 512:640].transpose(0, 2, 1, 3).reshape(DP, 2 * HD)
    grad_in = query_part + dot(grad_kv_own, kv_cols, 1, 1)
    normed_in, inverse_in = normed_all[2 * ROWS :], inverse_all[2 * ROWS :]
    input_grad = grad_resid + norm_back(normed_in, inverse_in, grad_in * gains[0:1], DM)
    grad_top = input_grad.astype(BF)
    grad_rest = (input_grad - grad_top.astype(F32)).astype(BF)
    input_grad = dot(grad_top, spread, 1, 1) + dot(grad_rest, spread, 1, 1)

    kv = total[:, 1024:]
    kv = jnp.concatenate(
        [kv] + [lax.ppermute(kv, "x", [(i, (i + s) % XS) for i in range(XS)]) for s in (3, 2, 1)],
        axis=1,
    )
    kv = jnp.concatenate([kv, kv], axis=1)
    kv = lax.dynamic_slice_in_dim(kv, ((XS - at) % XS) * 128, 512, 1)
    total = jnp.concatenate([total, kv], axis=1)
    mine = lax.dynamic_slice_in_dim(total, core * OWN, OWN, 0)
    other = lax.ppermute(lax.dynamic_slice_in_dim(total, (1 - core) * OWN, OWN, 0), "core", swap)
    left = jnp.where(core == 0, mine, other)
    right = jnp.where(core == 0, other, mine)

    def join(first, size):
        return jnp.concatenate([left[:, first : first + size], right[:, first : first + size]], 1)

    gains_total = right[:, 1024:1152]
    return (
        layer_out,
        input_grad,
        gains_total[:, 0],
        join(896, 128)[:, None, :],
        left[:, 1152:1408],
        left[:, 1408:1664],
        gains_total[:8, 4],
        gains_total[:8, 5],
        join(768, 128)[:, None, :],
        gains_total[:, 1],
        gains_total[:, 2],
        join(0, 256),
        join(256, 256),
        join(512, 256),
        gains_total[:, 3],
    )


def solution(mesh):
    fine = Mesh(mesh.devices.reshape(ZS, YS, CS, XS), EVERY)
    dp = ("z", "y", "core")
    in_specs = (
        P(EVERY, None),
        P(EVERY, None),
        P(dp),
        P(dp),
        P(dp, "x", None),
        P(dp, None),
        P(dp, None),
        P(dp),
        P(dp),
        P(dp, "x", None),
        P(dp),
        P(dp),
        P(dp, "x"),
        P(dp, "x"),
        P(dp, "x"),
        P(dp),
    )
    out_specs = (
        P(EVERY, None),
        P(EVERY, None),
        P(dp),
        P(dp, "x", None),
        P(dp, None),
        P(dp, None),
        P(dp),
        P(dp),
        P(dp, "x", None),
        P(dp),
        P(dp),
        P(dp, "x"),
        P(dp, "x"),
        P(dp, "x"),
        P(dp),
    )
    return jax.shard_map(
        per_device, mesh=fine, in_specs=in_specs, out_specs=out_specs, check_vma=False
    )
```

profile of v0, /device:TPU:3, one launch (start us, length us, event | category | flops | bytes accessed | tf_op | source)
XLA Modules:
  0.0 232.7 jit_solution(4319485971743457970)
XLA Ops:
  7.2 1.4 pad_maximum_fusion.4.wqo_ref
  8.6 1.4 convert_add_fusion.gains_ref
  10.0 1.7 shard_map.271
  11.7 3.8 %collective-permute-start = (bf16[256,640]{1,0:T(8,128)(2,1)}, bf16[256,640]{1,0:T(8,128)(2,1)S(1)}, u32[]{:S(2)}, u32[]{:S(2)}) collective-permute-start(bf16[256,640]{1,0:T(8,128)(2,1)} %param.16), channel_id=1, source_target_pairs={{0,2},{1,3},{4,6},{5,7},{8,10},{9,11},{12,14},{13,15},{16,18},{17,... | collective-permute-start | bytes 983048 | tf_op jit(solution)/shard_map/ppermute | solution.py:355
  15.5 1.9 collective-permute-start.1
  18.3 1.3 fusion.37
  19.6 1.3 fusion.38
  21.1 1.4 multiply_sine_fusion
  23.0 1.3 fusion.47.spread_ref
  24.2 1.9 fusion.15.heads_ref
  26.2 1.5 convolution_bitcast_fusion.up_ref
  27.7 4.3 %collective-permute-done.1 = bf16[256,640]{1,0:T(8,128)(2,1)S(1)} collective-permute-done((bf16[256,640]{1,0:T(8,128)(2,1)}, bf16[256,640]{1,0:T(8,128)(2,1)S(1)}, u32[]{:S(2)}, u32[]{:S(2)}) %collective-permute-start.1) | collective-permute-done | bytes 327712 | tf_op jit(solution)/shard_map/ppermute | solution.py:354
  32.0 2.6 %multiply_reduce_fusion = (f32[768]{0:T(1024)S(1)}, f32[768,768]{0,1:T(8,128)}) fusion(s32[768]{0:T(1024)S(1)} %get-tuple-element.99, s32[768]{0:T(1024)S(1)} %get-tuple-element.102, s32[768]{0:T(1024)S(1)} %get-tuple-element.100, s32[768]{0:T(1024)S(1)} %get-tuple-element.101, pred[768]{0:T(1024)(128)(4,1)S(1)} %get-tuple-element.103, ...), kind=kOutput, calls=%fused_computation.4 | convolution fusion | flops 762543360 | bytes 3359232 | tf_op jit(solution)/shard_map/dot_general | solution.py:54
  34.6 3.0 %copy.34 = f32[768,768]{1,0:T(8,128)} copy(f32[768,768]{0,1:T(8,128)} %get-tuple-element.96) | data formatting | bytes 4718592 | tf_op jit(solution)/shard_map/dot_general | solution.py:54
  37.6 1.2 slice.120.resid_ref
  38.8 3.3 %broadcast_multiply_fusion.normed_ref = f32[768,768]{1,0:T(8,128)} fusion(f32[768,768]{1,0:T(8,128)} %copy.34, f32[768]{0:T(1024)S(1)} %add_rsqrt_fusion), kind=kLoop, calls=%fused_computation.12 | loop fusion | flops 589824 | bytes 4721664 | tf_op jit(solution)/shard_map/mul | solution.py:38
  42.1 48.4 %all-gather.3.cloned.1.call-done = bf16[3072,2304]{1,0:T(8,128)(2,1)} async-done(((bf16[24,2304]{1,0:T(8,128)(2,1)}), bf16[3072,2304]{1,0:T(8,128)(2,1)}) %all-gather.3.cloned.1.call-update) | async-done | bytes 14155792 | tf_op jit(solution)/shard_map/all_gather | solution.py:352
  90.6 1.0 copy-done.8
  91.5 1.1 copy-done.14
  92.7 22.9 %shard_map.272 = (f32[16,768]{1,0:T(8,128)S(1)}, bf16[768,768]{1,0:T(8,128)(2,1)}, f32[256,1024]{1,0:T(8,128)}, f32[768,512]{1,0:T(8,128)}, bf16[256,1024]{1,0:T...) custom-call(s32[1]{0:T(128)} %bitcast.core_ref, ...), custom_call_target="tpu_custom_call" | custom-call | flops 10000000000 | bytes 20971520 | tf_op jit(solution)/shard_map/pallas_call | solution.py:303
  117.4 1.3 copy-done.4
  118.7 1.2 copy-done.5
  119.9 1.2 copy-done.6
  121.1 1.5 shard_map.273
  122.7 2.3 %collective-permute-done.2 = bf16[4,640,896]{2,1,0:T(8,128)(2,1)S(1)} collective-permute-done((bf16[4,640,896]{2,1,0:T(8,128)(2,1)}, bf16[4,640,896]{2,1,0:T(8,128)(2,1)S(1)}, u32[]{:S(2)}, u32[]{:S(2)}) %collective-permute-start.2) | collective-permute-done | bytes 4587552 | tf_op jit(solution)/shard_map/ppermute | solution.py:422
  125.1 3.2 %add_convert_fusion = bf16[4,640,896]{2,1,0:T(8,128)(2,1)} fusion(bf16[4,640,896]{2,1,0:T(8,128)(2,1)S(1)} %collective-permute-done.2, bf16[4,640,896]{2,1,0:T(8,128)(2,1)S(1)} %shard_map.273), kind=kLoop, calls=%fused_computation | loop fusion | flops 9175040 | bytes 13762560 | tf_op jit(solution)/shard_map/convert_element_type | solution.py:426
  128.3 1.4 fusion.22.heads_ref
  129.7 15.7 %shard_map.274 = (bf16[16,4,40,256]{3,2,1,0:T(8,128)(2,1)}, bf16[16,4,40,256]{3,2,1,0:T(8,128)(2,1)}, bf16[768,512]{1,0:T(8,128)(2,1)}, f32[256,768]{1,0:T(8,128)}) custom-call(s32[1]{0:T(128)} %bitcast.core_ref, bf16[32,4,24,2304]{3,2,1,0:T(8,128)(2,1)} %bitcast.28, bf16[256,768]{1,0:T(8,128)(2,1)} %copy-done.11, ...), custom_call_target="tpu_custom_call" | custom-call | flops 4000000000 | bytes 20971520 | tf_op jit(solution)/shard_map/pallas_call | solution.py:303
  145.7 1.9 fusion.50
  147.6 2.2 collective-permute-start.3
  149.8 1.6 collective-permute-start.4
  151.3 2.8 %add_convert_fusion.1 = bf16[16,4,40,256]{3,2,1,0:T(8,128)(2,1)} fusion(bf16[16,4,40,256]{3,2,1,0:T(8,128)(2,1)S(1)} %collective-permute-done.5, bf16[16,4,40,256]{3,2,1,0:T(8,128)(2,1)} %get-tuple-element.66), kind=kLoop, calls=%fused_computation.3 | loop fusion | flops 2621440 | bytes 3932160 | tf_op jit(solution)/shard_map/convert_element_type | solution.py:454
  154.2 6.3 %all-to-all-start = ((bf16[16,160,256]{2,1,0:T(8,128)(2,1)}), bf16[16,160,256]{2,1,0:T(8,128)(2,1)}, u32[]{:S(2)}, u32[]{:S(2)}) async-start(bf16[16,160,256]{2,1,0:T(8,128)(2,1)} %bitcast.13), calls=%async_computation | async-start | bytes 2621440 | tf_op jit(solution)/shard_map/all_to_all | solution.py:455
  160.5 1.4 slice_bitcast_fusion
  163.7 12.1 %collective-permute-done.4 = bf16[256,512]{1,0:T(8,128)(2,1)} collective-permute-done((bf16[256,512]{1,0:T(8,128)(2,1)}, bf16[256,512]{1,0:T(8,128)(2,1)}, u32[]{:S(2)}, u32[]{:S(2)}) %collective-permute-start.4) | collective-permute-done | bytes 262176 | tf_op jit(solution)/shard_map/ppermute | solution.py:453
  175.9 1.5 multiply_reduce_fusion.1
  177.4 1.1 multiply_add_fusion
  178.5 1.2 all-to-all-done
  179.8 7.8 %reduce-scatter.3.cloned.1.call-done = bf16[640,896]{1,0:T(8,128)(2,1)} async-done(((bf16[2560,896]{1,0:T(8,128)(2,1)}), bf16[640,896]{1,0:T(8,128)(2,1)}) %reduce-scatter.3.cloned.1.call-update) | async-done | bytes 1146896 | tf_op jit(solution)/shard_map/reduce_scatter | solution.py:428
  187.5 2.1 reduce_sum.52
  189.7 1.8 fusion.25
  191.5 6.9 %all-to-all-start.1 = ((bf16[16,40,896]{2,1,0:T(8,128)(2,1)}), bf16[16,40,896]{2,1,0:T(8,128)(2,1)S(1)}, u32[]{:S(2)}, u32[]{:S(2)}) async-start(bf16[16,40,896]{2,1,0:T(8,128)(2,1)} %bitcast.15), calls=%async_computation.2 | async-start | bytes 2293760 | tf_op jit(solution)/shard_map/all_to_all | solution.py:459
  198.4 10.1 %reduce-scatter.5.cloned.1.call-done = bf16[40,256]{1,0:T(8,128)(2,1)} async-done(((bf16[160,256]{1,0:T(8,128)(2,1)}), bf16[40,256]{1,0:T(8,128)(2,1)}) %reduce-scatter.5.cloned.1.call-update) | async-done | bytes 20496 | tf_op jit(solution)/shard_map/reduce_scatter | solution.py:458
  209.2 1.9 collective-permute-start.6
  211.6 1.4 collective-permute-start.8
  213.8 1.4 collective-permute-done.7
  215.7 3.7 %collective-permute-start.9 = (f32[20,1664]{1,0:T(8,128)S(1)}, f32[20,1664]{1,0:T(8,128)S(1)}, u32[]{:S(2)}, u32[]{:S(2)}) collective-permute-start(f32[20,1664]{1,0:T(8,128)S(1)} %constant_dynamic-slice_fusion), channel_id=1, source_target_pairs={{0,4},{4,0},{1,5},{5,1},{2,6},{6,2},{3,7},{7,3},{8,12},{12,8},{9,1... | collective-permute-start | bytes 399368 | tf_op jit(solution)/shard_map/ppermute | solution.py:483
  219.4 1.5 convolution_add_fusion.1
  (98 shorter events, 13.2 us)
Async XLA Ops:
  7.2 19.0 %copy-start = (bf16[256,640]{1,0:T(8,128)(2,1)S(1)}, bf16[256,640]{1,0:T(8,128)(2,1)}, u32[]{:S(2)}) copy-start(bf16[256,640]{1,0:T(8,128)(2,1)} %param.17) | copy-start | bytes 983044
  7.2 83.3 %all-gather.3.cloned.1.call-start = ((), (), s32[]{:S(2)}) async-start(), calls=%async_computation.6 | async-start | bytes 14266368 | tf_op jit(solution)/shard_map/all_gather | solution.py:352
  11.7 175.8 %reduce-scatter.3.cloned.1.call-start = ((), (), s32[]{:S(2)}) async-start(), calls=%async_computation.4 | async-start | bytes 5734400 | tf_op jit(solution)/shard_map/reduce_scatter | solution.py:428
  11.7 16.0 %collective-permute-start = (bf16[256,640]{1,0:T(8,128)(2,1)}, bf16[256,640]{1,0:T(8,128)(2,1)S(1)}, u32[]{:S(2)}, u32[]{:S(2)}) collective-permute-start(bf16[256,640]{1,0:T(8,128)(2,1)} %param.16), channel_id=1, source_target_pairs={{0,2},{1,3},{4,6},{5,7},{8,10},{9,11},{12,14},{13,15},{16,18},{17,... | collective-permute-start | bytes 983048 | tf_op jit(solution)/shard_map/ppermute | solution.py:355
  15.5 16.4 %collective-permute-start.1 = (bf16[256,640]{1,0:T(8,128)(2,1)}, bf16[256,640]{1,0:T(8,128)(2,1)S(1)}, u32[]{:S(2)}, u32[]{:S(2)}) collective-permute-start(bf16[256,640]{1,0:T(8,128)(2,1)} %param.16), channel_id=1, source_target_pairs={{0,1},{1,2},{2,3},{4,5},{5,6},{6,7},{8,9},{9,10},{10,11},{12,13},{... | collective-permute-start | bytes 983048 | tf_op jit(solution)/shard_map/ppermute | solution.py:354
  22.5 68.0 %copy-start.2 = (f32[768,128]{1,0:T(8,128)}, f32[768,128]{1,0:T(8,128)S(1)}, u32[]{:S(2)}) copy-start(f32[768,128]{1,0:T(8,128)S(1)} %get-tuple-element.93.sine_ref) | copy-start | bytes 1179652
  22.5 68.0 %copy-start.3 = (f32[768,128]{1,0:T(8,128)}, f32[768,128]{1,0:T(8,128)S(1)}, u32[]{:S(2)}) copy-start(f32[768,128]{1,0:T(8,128)S(1)} %get-tuple-element.94.cosine_ref) | copy-start | bytes 1179652
  26.2 5.8 %copy-start.18 = (bf16[256,640]{1,0:T(8,128)(2,1)S(1)}, bf16[256,640]{1,0:T(8,128)(2,1)}, u32[]{:S(2)}) copy-start(bf16[256,640]{1,0:T(8,128)(2,1)} %param.16) | copy-start | bytes 983044
  90.5 1.0 copy-start.8
  91.5 1.1 copy-start.14
  115.6 0.8 copy-start.7
  116.4 0.6 copy-start.12
  117.0 5.7 %copy-start.9 = (bf16[768,256]{1,0:T(8,128)(2,1)}, bf16[768,256]{1,0:T(8,128)(2,1)S(1)}, u32[]{:S(2)}) copy-start(bf16[768,256]{1,0:T(8,128)(2,1)S(1)} %get-tuple-element.59.k_ref) | copy-start | bytes 1179652
  117.0 5.7 %copy-start.10 = (bf16[768,256]{1,0:T(8,128)(2,1)}, bf16[768,256]{1,0:T(8,128)(2,1)S(1)}, u32[]{:S(2)}) copy-start(bf16[768,256]{1,0:T(8,128)(2,1)S(1)} %get-tuple-element.60.v_ref) | copy-start | bytes 1179652
  117.0 5.7 %copy-start.11 = (bf16[256,768]{1,0:T(8,128)(2,1)}, bf16[256,768]{1,0:T(8,128)(2,1)S(1)}, u32[]{:S(2)}) copy-start(bf16[256,768]{1,0:T(8,128)(2,1)S(1)} %get-tuple-element.54.dattn_ref) | copy-start | bytes 1179652
  117.0 5.7 %copy-start.13 = (f32[8,768]{1,0:T(8,128)}, f32[8,768]{1,0:T(8,128)S(1)}, u32[]{:S(2)}) copy-start(f32[8,768]{1,0:T(8,128)S(1)} %get-tuple-element.63.sums_ref) | copy-start | bytes 73732
  117.0 8.0 %collective-permute-start.2 = (bf16[4,640,896]{2,1,0:T(8,128)(2,1)}, bf16[4,640,896]{2,1,0:T(8,128)(2,1)S(1)}, u32[]{:S(2)}, u32[]{:S(2)}) collective-permute-start(bf16[4,640,896]{2,1,0:T(8,128)(2,1)} %get-tuple-element.52), channel_id=1, source_target_pairs={{0,4},{4,0},{1,5},{5,1},{2,6},{6,2},{3,7},{7,3},{8,12},{12,8},{9,1... | collective-permute-start | bytes 13762568 | tf_op jit(solution)/shard_map/ppermute | solution.py:422
  117.4 1.3 copy-start.4
  118.7 1.2 copy-start.5
  119.9 1.2 copy-start.6
  145.4 5.9 %collective-permute-start.5 = (bf16[16,4,40,256]{3,2,1,0:T(8,128)(2,1)}, bf16[16,4,40,256]{3,2,1,0:T(8,128)(2,1)S(1)}, u32[]{:S(2)}, u32[]{:S(2)}) collective-permute-start(bf16[16,4,40,256]{3,2,1,0:T(8,128)(2,1)} %get-tuple-element.67), channel_id=1, source_target_pairs={{0,4},{4,0},{1,5},{5,1},{2,6},{6,2},{3,7},{7,3},{8,12},{12,8},{9,1... | collective-permute-start | bytes 3932168 | tf_op jit(solution)/shard_map/ppermute | solution.py:449
  147.6 16.1 %collective-permute-start.3 = (bf16[256,512]{1,0:T(8,128)(2,1)}, bf16[256,512]{1,0:T(8,128)(2,1)S(1)}, u32[]{:S(2)}, u32[]{:S(2)}) collective-permute-start(bf16[256,512]{1,0:T(8,128)(2,1)} %get-tuple-element.77), channel_id=1, source_target_pairs={{1,0},{2,1},{3,2},{5,4},{6,5},{7,6},{9,8},{10,9},{11,10},{13,12},{... | collective-permute-start | bytes 786440 | tf_op jit(solution)/shard_map/ppermute | solution.py:450
  149.8 26.1 %collective-permute-start.4 = (bf16[256,512]{1,0:T(8,128)(2,1)}, bf16[256,512]{1,0:T(8,128)(2,1)}, u32[]{:S(2)}, u32[]{:S(2)}) collective-permute-start(bf16[256,512]{1,0:T(8,128)(2,1)} %get-tuple-element.78), channel_id=1, source_target_pairs={{2,0},{3,1},{6,4},{7,5},{10,8},{11,9},{14,12},{15,13},{18,16},{19,... | collective-permute-start | bytes 786440 | tf_op jit(solution)/shard_map/ppermute | solution.py:453
  154.2 25.6 %all-to-all-start = ((bf16[16,160,256]{2,1,0:T(8,128)(2,1)}), bf16[16,160,256]{2,1,0:T(8,128)(2,1)}, u32[]{:S(2)}, u32[]{:S(2)}) async-start(bf16[16,160,256]{2,1,0:T(8,128)(2,1)} %bitcast.13), calls=%async_computation | async-start | bytes 2621440 | tf_op jit(solution)/shard_map/all_to_all | solution.py:455
  160.5 15.4 %copy-start.15 = (f32[768,768]{1,0:T(8,128)S(1)}, f32[768,768]{1,0:T(8,128)}, u32[]{:S(2)}) copy-start(f32[768,768]{1,0:T(8,128)} %broadcast_multiply_fusion.normed_ref) | copy-start | bytes 7077892
  160.5 48.0 %reduce-scatter.5.cloned.1.call-start = ((), (), s32[]{:S(2)}) async-start(), calls=%async_computation.5 | async-start | bytes 102400 | tf_op jit(solution)/shard_map/reduce_scatter | solution.py:458
  160.5 15.3 %copy-start.16 = (f32[256,768]{1,0:T(8,128)S(1)}, f32[256,768]{1,0:T(8,128)}, u32[]{:S(2)}) copy-start(f32[256,768]{1,0:T(8,128)} %get-tuple-element.64) | copy-start | bytes 2359300
  191.5 27.9 %copy-start.17 = (f32[256,768]{1,0:T(8,128)S(1)}, f32[256,768]{1,0:T(8,128)}, u32[]{:S(2)}) copy-start(f32[256,768]{1,0:T(8,128)} %multiply_add_fusion) | copy-start | bytes 2359300
  191.5 24.0 %all-to-all-start.1 = ((bf16[16,40,896]{2,1,0:T(8,128)(2,1)}), bf16[16,40,896]{2,1,0:T(8,128)(2,1)S(1)}, u32[]{:S(2)}, u32[]{:S(2)}) async-start(bf16[16,40,896]{2,1,0:T(8,128)(2,1)} %bitcast.15), calls=%async_computation.2 | async-start | bytes 2293760 | tf_op jit(solution)/shard_map/all_to_all | solution.py:459
  209.2 4.6 %collective-permute-start.6 = (f32[40,128]{1,0:T(8,128)S(1)}, f32[40,128]{1,0:T(8,128)S(1)}, u32[]{:S(2)}, u32[]{:S(2)}) collective-permute-start(f32[40,128]{1,0:T(8,128)S(1)} %slice.123), channel_id=1, source_target_pairs={{0,3},{1,0},{2,1},{3,2},{4,7},{5,4},{6,5},{7,6},{8,11},{9,8},{10,9... | collective-permute-start | bytes 61448 | tf_op jit(solution)/shard_map/ppermute | solution.py:476
  211.1 4.1 %collective-permute-start.7 = (f32[40,128]{1,0:T(8,128)S(1)}, f32[40,128]{1,0:T(8,128)S(1)}, u32[]{:S(2)}, u32[]{:S(2)}) collective-permute-start(f32[40,128]{1,0:T(8,128)S(1)} %slice.123), channel_id=1, source_target_pairs={{0,2},{1,3},{2,0},{3,1},{4,6},{5,7},{6,4},{7,5},{8,10},{9,11},{10,... | collective-permute-start | bytes 61448 | tf_op jit(solution)/shard_map/ppermute | solution.py:476
  211.6 3.6 %collective-permute-start.8 = (f32[40,128]{1,0:T(8,128)S(1)}, f32[40,128]{1,0:T(8,128)S(1)}, u32[]{:S(2)}, u32[]{:S(2)}) collective-permute-start(f32[40,128]{1,0:T(8,128)S(1)} %slice.123), channel_id=1, source_target_pairs={{0,1},{1,2},{2,3},{3,0},{4,5},{5,6},{6,7},{7,4},{8,9},{9,10},{10,1... | collective-permute-start | bytes 61448 | tf_op jit(solution)/shard_map/ppermute | solution.py:476
  215.7 5.2 %collective-permute-start.9 = (f32[20,1664]{1,0:T(8,128)S(1)}, f32[20,1664]{1,0:T(8,128)S(1)}, u32[]{:S(2)}, u32[]{:S(2)}) collective-permute-start(f32[20,1664]{1,0:T(8,128)S(1)} %constant_dynamic-slice_fusion), channel_id=1, source_target_pairs={{0,4},{4,0},{1,5},{5,1},{2,6},{6,2},{3,7},{7,3},{8,12},{12,8},{9,1... | collective-permute-start | bytes 399368 | tf_op jit(solution)/shard_map/ppermute | solution.py:483
  219.4 6.8 %copy-start.1 = (bf16[256,640]{1,0:T(8,128)(2,1)S(1)}, bf16[256,640]{1,0:T(8,128)(2,1)}, u32[]{:S(2)}) copy-start(bf16[256,640]{1,0:T(8,128)(2,1)} %param.17) | copy-start | bytes 983044
Sparse Core Ops, SparseCore 0:
  11.8 78.6 all-gather.2
  128.4 59.1 reduce-scatter.2
  190.5 17.9 reduce-scatter.4
where the time goes:
time: 235 us; the launch traced here: 233 us
  waiting for transfers between devices  88.7 us (38%)
  Pallas kernels  41.8 us (18%)
  starting transfers between devices  30.9 us (13%)
  other arithmetic  27.4 us (12%)
  local copies, waits for them, and re-layouts  20.8 us (9%)
  between operations  14.2 us (6%)
  matrix products  9 us (4%)
    all_gather x1, waiting for transfers between devices, per_device(): lax.all_gather(packed, EVERY, axis=0, tiled=False)  48.4 us
    pallas_call x3, Pallas kernels, call(): pl.pallas_call(kernel, out_shape=[jax.ShapeDtypeStruct(shape, kind) for s...  40.2 us
    ppermute x1, waiting for transfers between devices, per_device(): lax.ppermute(grad_kv[:ROWS], 'x', [(i + 2, i) for i in range(XS - 2)])  12.1 us
    reduce_scatter x1, waiting for transfers between devices, per_device(): lax.psum_scatter(row_att, 'x', scatter_dimension=0, tiled=True).astype(F32)  10.1 us
    dot_general x5, matrix products, dot(): lax.dot_general(lhs, rhs, (((lhs_dim,), (rhs_dim,)), ((), ())), preferred...  9 us
    reduce_scatter x1, waiting for transfers between devices, per_device(): lax.psum_scatter(both_ff.reshape(XS * DM, 896), 'x', scatter_dimension=0,...  7.75 us
    unnamed x45, local copies, waits for them, and re-layouts  7.38 us
    all_to_all x1, starting transfers between devices, per_device(): lax.all_to_all(column_ff.reshape(16, 40, 896), ('z', 'y'), 0, 0, tiled=True)  6.86 us
  transfers between devices with their start and end apart: 15, of which 10 were waited for; matrix products, arithmetic and copies ran while one was open for 16% of the time, Pallas kernels for 7%

commit v1 on v0

--- a/solution.py
+++ b/solution.py
@@ -104,7 +104,7 @@
 def forward_kernel(
     core_ref, gathered, normed_ref, cosine_ref, sine_ref, bias_ref, heads_ref, resid_ref, up_ref,
     spread_ref,
-    gains_out, rows_out, qraw_out, kvraw_out, q_out, k_out, v_out, probs_out, mixed_out,
+    gains_out, qraw_out, kvraw_out, q_out, k_out, v_out, probs_out, mixed_out,
     layer_out, dres_out, dattn_out, away_out, sums_out, z_s, dg_s, du_s, rows_t_out, ff_t_out,
     attn_t_out, gate_s, upp_s, watt, sems, wff, ff_sems,
 ):
@@ -118,9 +118,8 @@
     gains_out[8:16] = jnp.concatenate([head_gains[0:8]] * 3, axis=1)
     query_gains, key_gains = head_gains[4:5], head_gains[5:6]
     rows = (normed_ref[...] * gains[0:1]).astype(BF)
-    rows_out[...] = rows
     kv_raw = dot(rows, kv_weights(watt), 1, 0)
-    kvraw_out[...] = kv_raw
+    kvraw_out[...] = kv_raw[:, :HD]
     key_norm, _ = norm_of(kv_raw[:, :HD], HD)
     key = rotate(key_norm * key_gains, cosine_ref[...], sine_ref[...]).astype(BF)
     value = kv_raw[:, HD:].astype(BF)
@@ -221,15 +220,16 @@
 
 
 def attend_back_kernel(
-    core_ref, gathered, dattn_ref, rows_ref, normed_ref, qraw_ref, kvraw_ref, q_ref, k_ref, v_ref,
+    core_ref, gathered, dattn_ref, normed_ref, qraw_ref, kvraw_ref, q_ref, k_ref, v_ref,
     probs_ref, cosine_ref, sine_ref, gains_ref, sums_ref, spread_ref, heads_ref,
-    keep_out, away_out, dkv_out, part_out, wq_s, wkv_s, watt, sems,
+    keep_out, away_out, dkv2_out, dkv1_out, dkv_out, part_out, wq_s, wkv_s, watt, sems,
 ):
     copies = fetch(gathered, watt, sems, 0, ATT)
     spread = spread_ref[...]
     query_gains, key_gains = gains_ref[12:13, :HD], gains_ref[13:14, :HD]
     grad_attn = dattn_ref[...]
-    rows_t = dot(spread, rows_ref[...], 1, 1).astype(BF)
+    rows = (normed_ref[...] * gains_ref[0:1]).astype(BF)
+    rows_t = dot(spread, rows, 1, 1).astype(BF)
     rows_own_t = rows_t[:, 2 * ROWS :]
     key, value = k_ref[...], v_ref[...]
     cosine, sine = cosine_ref[2 * ROWS :], sine_ref[2 * ROWS :]
@@ -258,12 +258,14 @@
         part = part + dot(grad_raw, cut(watt, head, 0, 256), 1, 1)
         wq_s[:, at] = dot(rows_own_t, grad_raw, 1, 0).astype(BF)
     part_out[...] = part
-    key_norm, key_inv = norm_of(kvraw_ref[:, :HD], HD)
+    key_norm, key_inv = norm_of(kvraw_ref[...], HD)
     grad_key = rotate(grad_key * SCALE, cosine_ref[...], -sine_ref[...])
     grad_gk = jnp.sum(grad_key * key_norm, axis=0, keepdims=True)
     grad_key = norm_back(key_norm, key_inv, grad_key * key_gains, HD)
     grad_kv = jnp.concatenate([grad_key, grad_value], axis=1).astype(BF)
-    dkv_out[...] = grad_kv
+    dkv2_out[...] = grad_kv[:ROWS]
+    dkv1_out[...] = grad_kv[ROWS : 2 * ROWS]
+    dkv_out[...] = grad_kv[2 * ROWS :]
     wkv_s[...] = dot(rows_t, grad_kv, 1, 0).astype(BF)
     kv_part = dot(grad_kv, kv_weights(watt), 1, 1)
     grad_gin = jnp.sum(kv_part * normed_ref[...], axis=0, keepdims=True)
@@ -287,6 +289,22 @@
         sent = jnp.where(own_kv, gains.astype(F32), kv).reshape(16, 40, 128).astype(BF)
         keep_out[:, x, :, 128:256] = kept
         away_out[:, x, :, 128:256] = sent
+
+
+def final_kernel(core_ref, total_ref, other_ref, wq, wo, wg, wu, wd, wk, wv, *gain_refs):
+    first = jnp.broadcast_to(core_ref[0], (OWN, total_ref.shape[1])) == 0
+    mine = jnp.where(first, total_ref[0:OWN], total_ref[OWN : 2 * OWN])
+    other = other_ref[...]
+    left = jnp.where(first, mine, other)
+    right = jnp.where(first, other, mine)
+    for ref, at, size in ((wg, 0, 256), (wu, 256, 256), (wd, 512, 256), (wo, 768, 128), (wq, 896, 128)):
+        ref[:, :size] = left[:, at : at + size]
+        ref[:, size:] = right[:, at : at + size]
+    wk[...] = left[:, 1152:1408]
+    wv[...] = left[:, 1408:1664]
+    gains = jnp.concatenate([right[:, 1024:1152], jnp.zeros((PAD - OWN, 128), F32)], axis=0).T
+    for row, ref in enumerate(gain_refs):
+        ref[...] = gains[row : row + 1, : ref.shape[1]]
 
 
 def call(kernel, outs, args, scratch=(), word=None, weights=None, flops=0, vmem=0):
@@ -384,16 +402,17 @@
     bias = jnp.where(visible, 0.0, NEGATIVE).astype(F32)
 
     core_word = core.astype(jnp.int32).reshape(1)
+    head_rows = head_matrix(OWN)
+    core_word, head_rows = lax.optimization_barrier((core_word, head_rows))
     (
-        gains, rows_all, query_raw, kv_raw, query, key, value, probs, mixed,
+        gains, query_raw, kv_raw, query, key, value, probs, mixed,
         layer_out, grad_resid, grad_attn, away_ff, sums, *feed,
     ) = call(
         forward_kernel,
         [
             ((16, DP), F32),
-            ((KEYS, DP), BF),
             ((ROWS, HQ * HD), F32),
-            ((KEYS, 2 * HD), F32),
+            ((KEYS, HD), F32),
             ((ROWS, HQ * HD), BF),
             ((KEYS, HD), BF),
             ((KEYS, HD), BF),
@@ -428,17 +447,19 @@
     column_ff = lax.psum_scatter(
         both_ff.reshape(XS * DM, 896), "x", scatter_dimension=0, tiled=True
     )
-    keep_att, away_att, grad_kv, query_part = call(
+    keep_att, away_att, grad_kv_two, grad_kv_one, grad_kv, query_part = call(
         attend_back_kernel,
         [
             ((16, XS, 40, 256), BF),
             ((16, XS, 40, 256), BF),
-            ((KEYS, 2 * HD), BF),
+            ((ROWS, 2 * HD), BF),
+            ((ROWS, 2 * HD), BF),
+            ((ROWS, 2 * HD), BF),
             ((ROWS, DP), F32),
         ],
         [
-            grad_attn, rows_all, normed_all, query_raw, kv_raw, query, key, value, probs,
-            cosine, sine, gains, sums, spread, head_matrix(OWN),
+            grad_attn, normed_all, query_raw, kv_raw, query, key, value, probs,
+            cosine, sine, gains, sums, spread, head_rows,
         ],
         [((DM, 1024), BF), ((DM, 512), BF)],
         word=core_word,
@@ -448,20 +469,26 @@
     )
     arrived_att = lax.ppermute(away_att, "core", swap)
     from_one = lax.ppermute(
-        grad_kv[ROWS : 2 * ROWS], "x", [(i + 1, i) for i in range(XS - 1)]
-    )
-    from_two = lax.ppermute(grad_kv[:ROWS], "x", [(i + 2, i) for i in range(XS - 2)])
+        grad_kv_one, "x", [(i + 1, i) for i in range(XS - 1)]
+    )
+    from_two = lax.ppermute(grad_kv_two, "x", [(i + 2, i) for i in range(XS - 2)])
     both_att = (keep_att.astype(F32) + arrived_att.astype(F32)).astype(BF)
     parts_att = lax.all_to_all(both_att.reshape(16, 160, 256), ("z", "y"), 0, 0, tiled=True)
     parts_att, column_ff = lax.optimization_barrier((parts_att, column_ff))
     row_att = jnp.sum(parts_att.astype(F32), axis=0).astype(BF)
-    total_att = lax.psum_scatter(row_att, "x", scatter_dimension=0, tiled=True).astype(F32)
+    one, two, three = (
+        lax.ppermute(row_att, "x", [(i, (i + step) % XS) for i in range(XS)]).astype(F32)
+        for step in (1, 2, 3)
+    )
+    all_att = ((row_att.astype(F32) + two) + (one + three)).reshape(XS, 40, 256)
+    total_att = lax.dynamic_index_in_dim(all_att, at, 0, keepdims=False)
+    total_kv = all_att[:, :, 128:].transpose(1, 0, 2).reshape(40, 512)
     parts_ff = lax.all_to_all(column_ff.reshape(16, 40, 896), ("z", "y"), 0, 0, tiled=True)
     total_ff = jnp.sum(parts_ff.astype(F32), axis=0)
-    total = jnp.concatenate([total_ff, total_att], axis=1)
+    total = jnp.concatenate([total_ff, total_att, total_kv], axis=1)
 
     grad_kv_own = (
-        grad_kv[2 * ROWS :].astype(F32) + from_one.astype(F32) + from_two.astype(F32)
+        grad_kv.astype(F32) + from_one.astype(F32) + from_two.astype(F32)
     ).astype(BF)
     kv_cols = gathered[:, :, :, 512:640].transpose(0, 2, 1, 3).reshape(DP, 2 * HD)
     grad_in = query_part + dot(grad_kv_own, kv_cols, 1, 1)
@@ -471,39 +498,29 @@
     grad_rest = (input_grad - grad_top.astype(F32)).astype(BF)
     input_grad = dot(grad_top, spread, 1, 1) + dot(grad_rest, spread, 1, 1)
 
-    kv = total[:, 1024:]
-    kv = jnp.concatenate(
-        [kv] + [lax.ppermute(kv, "x", [(i, (i + s) % XS) for i in range(XS)]) for s in (3, 2, 1)],
-        axis=1,
-    )
-    kv = jnp.concatenate([kv, kv], axis=1)
-    kv = lax.dynamic_slice_in_dim(kv, ((XS - at) % XS) * 128, 512, 1)
-    total = jnp.concatenate([total, kv], axis=1)
-    mine = lax.dynamic_slice_in_dim(total, core * OWN, OWN, 0)
     other = lax.ppermute(lax.dynamic_slice_in_dim(total, (1 - core) * OWN, OWN, 0), "core", swap)
-    left = jnp.where(core == 0, mine, other)
-    right = jnp.where(core == 0, other, mine)
-
-    def join(first, size):
-        return jnp.concatenate([left[:, first : first + size], right[:, first : first + size]], 1)
-
-    gains_total = right[:, 1024:1152]
+    outs = [(OWN, 256), (OWN, 256), (OWN, 512), (OWN, 512), (OWN, 512), (OWN, 256), (OWN, 256)]
+    outs += [(1, OWN)] * 4 + [(1, 8)] * 2
+    grad_wq, grad_wo, grad_wg, grad_wu, grad_wd, grad_wk, grad_wv, *grad_gains = call(
+        final_kernel, [(shape, F32) for shape in outs], [total, other], word=core_word, vmem=16
+    )
+    grad_gains = [grad[0] for grad in grad_gains]
     return (
         layer_out,
         input_grad,
-        gains_total[:, 0],
-        join(896, 128)[:, None, :],
-        left[:, 1152:1408],
-        left[:, 1408:1664],
-        gains_total[:8, 4],
-        gains_total[:8, 5],
-        join(768, 128)[:, None, :],
-        gains_total[:, 1],
-        gains_total[:, 2],
-        join(0, 256),
-        join(256, 256),
-        join(512, 256),
-        gains_total[:, 3],
+        grad_gains[0],
+        grad_wq[:, None, :],
+        grad_wk,
+        grad_wv,
+        grad_gains[4],
+        grad_gains[5],
+        grad_wo[:, None, :],
+        grad_gains[1],
+        grad_gains[2],
+        grad_wg,
+        grad_wu,
+        grad_wd,
+        grad_gains[3],
     )
 
 

time: 235 us -> 227 us (0.966)
  local copies, waits for them, and re-layouts: 20.8 us -> 15.8 us
    reduce_scatter x1 -> x0, waiting for transfers between devices: 10.1 us -> none  [per_device(): lax.psum_scatter(row_att, 'x', scatter_dimension=0, tiled=True).astype(F32)]
    ppermute x5, waiting for transfers between devices: 14.3 us -> 23.4 us  [the longest x1 12 us: per_device(): lax.ppermute(grad_kv_two, 'x', [(i + 2, i) for i in range(XS - 2)])]
    all_to_all x1, waiting for transfers between devices: 0.19 us -> 6.45 us  [per_device(): lax.all_to_all(column_ff.reshape(16, 40, 896), ('z', 'y'), 0, 0, tiled=True)]
    slice x8 -> x0, local copies, waits for them, and re-layouts: 4.66 us -> none  [the longest x1 1.86 us: per_device(): grad_kv[ROWS:2 * ROWS]]
    reduce_scatter x1, waiting for transfers between devices: 7.75 us -> 3.15 us  [per_device(): lax.psum_scatter(both_ff.reshape(XS * DM, 896), 'x', scatter_dimension=0,...]
    ppermute x1, waiting for transfers between devices: 0.01 us -> 2.99 us  [per_device(): arrived_att = lax.ppermute(away_att, 'core', swap)]
    unnamed x45 -> x42, local copies, waits for them, and re-layouts: 7.38 us -> 8.42 us
    pallas_call x3 -> x4, Pallas kernels: 40.2 us -> 40.1 us  [call(): pl.pallas_call(kernel, out_shape=[jax.ShapeDtypeStruct(shape, kind) for s...]
  transfers between devices with their start and end apart: 15 -> 14, of which waited for: 10 -> 11; matrix products, arithmetic and copies ran while one was open for 16% -> 16% of each run, Pallas kernels for 7% -> 7%
where the time goes in v1:
time: 227 us; the launch traced here: 226 us
  waiting for transfers between devices  89.6 us (39%)
  Pallas kernels  41.8 us (18%)
  starting transfers between devices  28.9 us (13%)
  other arithmetic  26.7 us (12%)
  local copies, waits for them, and re-layouts  15.8 us (7%)
  between operations  14.4 us (6%)
  matrix products  8.77 us (4%)
    all_gather x1, waiting for transfers between devices, per_device(): lax.all_gather(packed, EVERY, axis=0, tiled=False)  48.4 us
    pallas_call x4, Pallas kernels, call(): pl.pallas_call(kernel, out_shape=[jax.ShapeDtypeStruct(shape, kind) for s...  40.1 us
    ppermute x1, waiting for transfers between devices, per_device(): lax.ppermute(grad_kv_two, 'x', [(i + 2, i) for i in range(XS - 2)])  12 us
    ppermute x1, waiting for transfers between devices, per_device(): lax.ppermute(grad_kv_one, 'x', [(i + 1, i) for i in range(XS - 1)])  8.97 us
    dot_general x5, matrix products, dot(): lax.dot_general(lhs, rhs, (((lhs_dim,), (rhs_dim,)), ((), ())), preferred...  8.77 us
    unnamed x42, local copies, waits for them, and re-layouts  8.42 us
    all_to_all x1, starting transfers between devices, per_device(): lax.all_to_all(column_ff.reshape(16, 40, 896), ('z', 'y'), 0, 0, tiled=True)  6.75 us
    all_to_all x1, waiting for transfers between devices, per_device(): lax.all_to_all(column_ff.reshape(16, 40, 896), ('z', 'y'), 0, 0, tiled=True)  6.45 us
  transfers between devices with their start and end apart: 14, of which 11 were waited for; matrix products, arithmetic and copies ran while one was open for 16% of the time, Pallas kernels for 7%

profile of v1, /device:TPU:3, one launch (start us, length us, event | category | flops | bytes accessed | tf_op | source)
XLA Modules:
  0.0 225.9 jit_solution(3661662421013956944)
XLA Ops:
  7.2 1.4 pad_maximum_fusion.1.wqo_ref
  8.6 1.4 convert_add_fusion.gains_ref
  10.0 1.7 shard_map.271
  11.7 3.8 %collective-permute-start = (bf16[256,640]{1,0:T(8,128)(2,1)}, bf16[256,640]{1,0:T(8,128)(2,1)S(1)}, u32[]{:S(2)}, u32[]{:S(2)}) collective-permute-start(bf16[256,640]{1,0:T(8,128)(2,1)} %param.16), channel_id=1, source_target_pairs={{0,2},{1,3},{4,6},{5,7},{8,10},{9,11},{12,14},{13,15},{16,18},{17,... | collective-permute-start | bytes 983048 | tf_op jit(solution)/shard_map/ppermute | solution.py:373
  15.5 1.9 collective-permute-start.1
  18.3 1.3 fusion.36
  19.6 1.3 fusion.37
  21.1 1.9 fusion.15.heads_ref
  23.0 1.4 multiply_sine_fusion
  24.9 1.3 fusion.46.spread_ref
  26.2 1.4 fusion.22.heads_ref
  27.6 1.5 convolution_bitcast_fusion.up_ref
  29.1 2.8 %collective-permute-done.1 = bf16[256,640]{1,0:T(8,128)(2,1)S(1)} collective-permute-done((bf16[256,640]{1,0:T(8,128)(2,1)}, bf16[256,640]{1,0:T(8,128)(2,1)S(1)}, u32[]{:S(2)}, u32[]{:S(2)}) %collective-permute-start.1) | collective-permute-done | bytes 327712 | tf_op jit(solution)/shard_map/ppermute | solution.py:372
  32.0 2.6 %multiply_reduce_fusion = (f32[768]{0:T(1024)S(1)}, f32[768,768]{0,1:T(8,128)}) fusion(s32[768]{0:T(1024)S(1)} %get-tuple-element.151, s32[768]{0:T(1024)S(1)} %get-tuple-element.154, s32[768]{0:T(1024)S(1)} %get-tuple-element.152, s32[768]{0:T(1024)S(1)} %get-tuple-element.153, pred[768]{0:T(1024)(128)(4,1)S(1)} %get-tuple-element.155, ...), kind=kOutput, calls=%fused_computation.4 | convolution fusion | flops 762543360 | bytes 3359232 | tf_op jit(solution)/shard_map/dot_general | solution.py:54
  34.6 3.1 %copy.36 = f32[768,768]{1,0:T(8,128)} copy(f32[768,768]{0,1:T(8,128)} %get-tuple-element.136) | data formatting | bytes 4718592 | tf_op jit(solution)/shard_map/dot_general | solution.py:54
  37.6 1.2 slice.29.resid_ref
  38.8 3.3 %broadcast_multiply_fusion.normed_ref = f32[768,768]{1,0:T(8,128)} fusion(f32[768,768]{1,0:T(8,128)} %copy.36, f32[768]{0:T(1024)S(1)} %add_rsqrt_fusion), kind=kLoop, calls=%fused_computation.12 | loop fusion | flops 589824 | bytes 4721664 | tf_op jit(solution)/shard_map/mul | solution.py:38
  42.1 48.4 %all-gather.3.cloned.1.call-done = bf16[3072,2304]{1,0:T(8,128)(2,1)} async-done(((bf16[24,2304]{1,0:T(8,128)(2,1)}), bf16[3072,2304]{1,0:T(8,128)(2,1)}) %all-gather.3.cloned.1.call-update) | async-done | bytes 14155792 | tf_op jit(solution)/shard_map/all_gather | solution.py:370
  90.6 1.0 copy-done.9
  91.6 22.9 %shard_map.272 = (f32[16,768]{1,0:T(8,128)S(1)}, f32[256,1024]{1,0:T(8,128)}, f32[768,256]{1,0:T(8,128)S(1)}, bf16[256,1024]{1,0:T(8,128)(2,1)S(1)}, bf16[768,25...) custom-call(s32[1]{0:T(128)} %bitcast.core_ref, ...), custom_call_target="tpu_custom_call" | custom-call | flops 10000000000 | bytes 20971520 | tf_op jit(solution)/shard_map/pallas_call | solution.py:321
  117.3 1.2 copy-done.4
  118.5 1.2 copy-done.5
  119.7 1.2 copy-done.6
  120.9 1.5 shard_map.273
  122.5 2.4 %collective-permute-done.2 = bf16[4,640,896]{2,1,0:T(8,128)(2,1)S(1)} collective-permute-done((bf16[4,640,896]{2,1,0:T(8,128)(2,1)}, bf16[4,640,896]{2,1,0:T(8,128)(2,1)S(1)}, u32[]{:S(2)}, u32[]{:S(2)}) %collective-permute-start.2) | collective-permute-done | bytes 4587552 | tf_op jit(solution)/shard_map/ppermute | solution.py:441
  124.9 3.2 %add_convert_fusion = bf16[4,640,896]{2,1,0:T(8,128)(2,1)} fusion(bf16[4,640,896]{2,1,0:T(8,128)(2,1)S(1)} %collective-permute-done.2, bf16[4,640,896]{2,1,0:T(8,128)(2,1)S(1)} %shard_map.273), kind=kLoop, calls=%fused_computation | loop fusion | flops 9175040 | bytes 13762560 | tf_op jit(solution)/shard_map/convert_element_type | solution.py:445
  128.1 15.0 %shard_map.274 = (bf16[16,4,40,256]{3,2,1,0:T(8,128)(2,1)}, bf16[16,4,40,256]{3,2,1,0:T(8,128)(2,1)}, bf16[256,512]{1,0:T(8,128)(2,1)}, bf16[256,512]{1,0:T(8,12...) custom-call(s32[1]{0:T(128)} %bitcast.core_ref, bf16[32,4,24,2304]{3,2,1,0:T(8,128)(2,1)} %bitcast.47, ...), custom_call_target="tpu_custom_call" | custom-call | flops 4000000000 | bytes 20971520 | tf_op jit(solution)/shard_map/pallas_call | solution.py:321
  143.4 3.0 %collective-permute-done.5 = bf16[16,4,40,256]{3,2,1,0:T(8,128)(2,1)S(1)} collective-permute-done((bf16[16,4,40,256]{3,2,1,0:T(8,128)(2,1)}, bf16[16,4,40,256]{3,2,1,0:T(8,128)(2,1)S(1)}, u32[]{:S(2)}, u32[]{:S(2)}) %collective-permute-start.5) | collective-permute-done | bytes 1310752 | tf_op jit(solution)/shard_map/ppermute | solution.py:470
  146.4 2.9 %add_convert_fusion.1 = bf16[16,4,40,256]{3,2,1,0:T(8,128)(2,1)} fusion(bf16[16,4,40,256]{3,2,1,0:T(8,128)(2,1)S(1)} %collective-permute-done.5, bf16[16,4,40,256]{3,2,1,0:T(8,128)(2,1)} %get-tuple-element.85), kind=kLoop, calls=%fused_computation.3 | loop fusion | flops 2621440 | bytes 3932160 | tf_op jit(solution)/shard_map/convert_element_type | solution.py:475
  149.3 5.2 %all-to-all-start = ((bf16[16,160,256]{2,1,0:T(8,128)(2,1)}), bf16[16,160,256]{2,1,0:T(8,128)(2,1)}, u32[]{:S(2)}, u32[]{:S(2)}) async-start(bf16[16,160,256]{2,1,0:T(8,128)(2,1)} %bitcast.13), calls=%async_computation | async-start | bytes 2621440 | tf_op jit(solution)/shard_map/all_to_all | solution.py:476
  154.5 3.8 %collective-permute-start.3 = (bf16[256,512]{1,0:T(8,128)(2,1)}, bf16[256,512]{1,0:T(8,128)(2,1)S(1)}, u32[]{:S(2)}, u32[]{:S(2)}) collective-permute-start(bf16[256,512]{1,0:T(8,128)(2,1)} %get-tuple-element.83), channel_id=1, source_target_pairs={{1,0},{2,1},{3,2},{5,4},{6,5},{7,6},{9,8},{10,9},{11,10},{13,12},{... | collective-permute-start | bytes 786440 | tf_op jit(solution)/shard_map/ppermute | solution.py:471
  158.3 1.3 collective-permute-start.4
  159.6 1.2 slice_bitcast_fusion
  161.9 9.0 %collective-permute-done.3 = bf16[256,512]{1,0:T(8,128)(2,1)S(1)} collective-permute-done((bf16[256,512]{1,0:T(8,128)(2,1)}, bf16[256,512]{1,0:T(8,128)(2,1)S(1)}, u32[]{:S(2)}, u32[]{:S(2)}) %collective-permute-start.3) | collective-permute-done | bytes 262176 | tf_op jit(solution)/shard_map/ppermute | solution.py:471
  170.8 12.0 %collective-permute-done.4 = bf16[256,512]{1,0:T(8,128)(2,1)S(1)} collective-permute-done((bf16[256,512]{1,0:T(8,128)(2,1)}, bf16[256,512]{1,0:T(8,128)(2,1)S(1)}, u32[]{:S(2)}, u32[]{:S(2)}) %collective-permute-start.4) | collective-permute-done | bytes 262176 | tf_op jit(solution)/shard_map/ppermute | solution.py:474
  182.9 1.3 multiply_reduce_fusion.1
  184.2 3.2 %reduce-scatter.2.cloned.1.call-done = bf16[640,896]{1,0:T(8,128)(2,1)} async-done(((bf16[2560,896]{1,0:T(8,128)(2,1)}), bf16[640,896]{1,0:T(8,128)(2,1)}) %reduce-scatter.2.cloned.1.call-update) | async-done | bytes 1146896 | tf_op jit(solution)/shard_map/reduce_scatter | solution.py:447
  187.4 6.8 %all-to-all-start.1 = ((bf16[16,40,896]{2,1,0:T(8,128)(2,1)}), bf16[16,40,896]{2,1,0:T(8,128)(2,1)}, u32[]{:S(2)}, u32[]{:S(2)}) async-start(bf16[16,40,896]{2,1,0:T(8,128)(2,1)} %bitcast.50), calls=%async_computation.2 | async-start | bytes 2293760 | tf_op jit(solution)/shard_map/all_to_all | solution.py:486
  194.2 2.2 multiply_add_fusion
  196.4 1.5 reduce_sum.52
  198.0 0.9 collective-permute-start.7
  198.9 1.7 collective-permute-start.8
  200.6 1.8 fusion.24
  203.2 0.9 collective-permute-done.7
  204.9 6.5 %all-to-all-done.1 = bf16[16,40,896]{2,1,0:T(8,128)(2,1)} async-done(((bf16[16,40,896]{2,1,0:T(8,128)(2,1)}), bf16[16,40,896]{2,1,0:T(8,128)(2,1)}, u32[]{:S(2)}, u32[]{:S(2)}) %all-to-all-start.1) | async-done | bytes 1146912 | tf_op jit(solution)/shard_map/all_to_all | solution.py:486
  211.3 1.4 convert_reduce_fusion
  212.8 2.8 %collective-permute-start.9 = (f32[20,1664]{1,0:T(8,128)S(1)}, f32[20,1664]{1,0:T(8,128)S(1)}, u32[]{:S(2)}, u32[]{:S(2)}) collective-permute-start(f32[20,1664]{1,0:T(8,128)S(1)} %constant_dynamic-slice_fusion), channel_id=1, source_target_pairs={{0,4},{4,0},{1,5},{5,1},{2,6},{6,2},{3,7},{7,3},{8,12},{12,8},{9,1... | collective-permute-start | bytes 399368 | tf_op jit(solution)/shard_map/ppermute | solution.py:501
  215.6 1.5 convolution_add_fusion.1
  (77 shorter events, 9.3 us)
Async XLA Ops:
  7.2 20.4 %copy-start = (bf16[256,640]{1,0:T(8,128)(2,1)S(1)}, bf16[256,640]{1,0:T(8,128)(2,1)}, u32[]{:S(2)}) copy-start(bf16[256,640]{1,0:T(8,128)(2,1)} %param.17) | copy-start | bytes 983044
  7.2 83.4 %all-gather.3.cloned.1.call-start = ((), (), s32[]{:S(2)}) async-start(), calls=%async_computation.4 | async-start | bytes 14266368 | tf_op jit(solution)/shard_map/all_gather | solution.py:370
  11.7 175.7 %reduce-scatter.2.cloned.1.call-start = ((), (), s32[]{:S(2)}) async-start(), calls=%async_computation.3 | async-start | bytes 5734400 | tf_op jit(solution)/shard_map/reduce_scatter | solution.py:447
  11.7 17.4 %collective-permute-start = (bf16[256,640]{1,0:T(8,128)(2,1)}, bf16[256,640]{1,0:T(8,128)(2,1)S(1)}, u32[]{:S(2)}, u32[]{:S(2)}) collective-permute-start(bf16[256,640]{1,0:T(8,128)(2,1)} %param.16), channel_id=1, source_target_pairs={{0,2},{1,3},{4,6},{5,7},{8,10},{9,11},{12,14},{13,15},{16,18},{17,... | collective-permute-start | bytes 983048 | tf_op jit(solution)/shard_map/ppermute | solution.py:373
  15.5 16.4 %collective-permute-start.1 = (bf16[256,640]{1,0:T(8,128)(2,1)}, bf16[256,640]{1,0:T(8,128)(2,1)S(1)}, u32[]{:S(2)}, u32[]{:S(2)}) collective-permute-start(bf16[256,640]{1,0:T(8,128)(2,1)} %param.16), channel_id=1, source_target_pairs={{0,1},{1,2},{2,3},{4,5},{5,6},{6,7},{8,9},{9,10},{10,11},{12,13},{... | collective-permute-start | bytes 983048 | tf_op jit(solution)/shard_map/ppermute | solution.py:372
  24.5 66.1 %copy-start.2 = (f32[768,128]{1,0:T(8,128)}, f32[768,128]{1,0:T(8,128)S(1)}, u32[]{:S(2)}) copy-start(f32[768,128]{1,0:T(8,128)S(1)} %get-tuple-element.133.sine_ref) | copy-start | bytes 1179652
  24.5 66.1 %copy-start.3 = (f32[768,128]{1,0:T(8,128)}, f32[768,128]{1,0:T(8,128)S(1)}, u32[]{:S(2)}) copy-start(f32[768,128]{1,0:T(8,128)S(1)} %get-tuple-element.134.cosine_ref) | copy-start | bytes 1179652
  27.6 4.4 %copy-start.19 = (bf16[256,640]{1,0:T(8,128)(2,1)S(1)}, bf16[256,640]{1,0:T(8,128)(2,1)}, u32[]{:S(2)}) copy-start(bf16[256,640]{1,0:T(8,128)(2,1)} %param.16) | copy-start | bytes 983044
  90.6 1.0 copy-start.9
  114.5 0.9 copy-start.7
  115.4 0.8 copy-start.8
  116.2 0.8 copy-start.11
  116.9 5.6 %copy-start.10 = (bf16[768,256]{1,0:T(8,128)(2,1)}, bf16[768,256]{1,0:T(8,128)(2,1)S(1)}, u32[]{:S(2)}) copy-start(bf16[768,256]{1,0:T(8,128)(2,1)S(1)} %get-tuple-element.75.k_ref) | copy-start | bytes 1179652
  116.9 5.6 %copy-start.12 = (bf16[256,768]{1,0:T(8,128)(2,1)}, bf16[256,768]{1,0:T(8,128)(2,1)S(1)}, u32[]{:S(2)}) copy-start(bf16[256,768]{1,0:T(8,128)(2,1)S(1)} %get-tuple-element.71.dattn_ref) | copy-start | bytes 1179652
  116.9 5.6 %copy-start.13 = (f32[16,768]{1,0:T(8,128)}, f32[16,768]{1,0:T(8,128)S(1)}, u32[]{:S(2)}) copy-start(f32[16,768]{1,0:T(8,128)S(1)} %get-tuple-element.78.gains_ref) | copy-start | bytes 147460
  116.9 5.6 %copy-start.14 = (f32[8,768]{1,0:T(8,128)}, f32[8,768]{1,0:T(8,128)S(1)}, u32[]{:S(2)}) copy-start(f32[8,768]{1,0:T(8,128)S(1)} %get-tuple-element.79.sums_ref) | copy-start | bytes 73732
  116.9 8.0 %collective-permute-start.2 = (bf16[4,640,896]{2,1,0:T(8,128)(2,1)}, bf16[4,640,896]{2,1,0:T(8,128)(2,1)S(1)}, u32[]{:S(2)}, u32[]{:S(2)}) collective-permute-start(bf16[4,640,896]{2,1,0:T(8,128)(2,1)} %get-tuple-element.69), channel_id=1, source_target_pairs={{0,4},{4,0},{1,5},{5,1},{2,6},{6,2},{3,7},{7,3},{8,12},{12,8},{9,1... | collective-permute-start | bytes 13762568 | tf_op jit(solution)/shard_map/ppermute | solution.py:441
  117.3 1.2 copy-start.4
  118.5 1.2 copy-start.5
  119.7 1.2 copy-start.6
  143.1 3.3 %collective-permute-start.5 = (bf16[16,4,40,256]{3,2,1,0:T(8,128)(2,1)}, bf16[16,4,40,256]{3,2,1,0:T(8,128)(2,1)S(1)}, u32[]{:S(2)}, u32[]{:S(2)}) collective-permute-start(bf16[16,4,40,256]{3,2,1,0:T(8,128)(2,1)} %get-tuple-element.86), channel_id=1, source_target_pairs={{0,4},{4,0},{1,5},{5,1},{2,6},{6,2},{3,7},{7,3},{8,12},{12,8},{9,1... | collective-permute-start | bytes 3932168 | tf_op jit(solution)/shard_map/ppermute | solution.py:470
  149.3 33.6 %copy-start.18 = (bf16[256,512]{1,0:T(8,128)(2,1)S(1)}, bf16[256,512]{1,0:T(8,128)(2,1)}, u32[]{:S(2)}) copy-start(bf16[256,512]{1,0:T(8,128)(2,1)} %get-tuple-element.82) | copy-start | bytes 786436
  149.3 34.9 %all-to-all-start = ((bf16[16,160,256]{2,1,0:T(8,128)(2,1)}), bf16[16,160,256]{2,1,0:T(8,128)(2,1)}, u32[]{:S(2)}, u32[]{:S(2)}) async-start(bf16[16,160,256]{2,1,0:T(8,128)(2,1)} %bitcast.13), calls=%async_computation | async-start | bytes 2621440 | tf_op jit(solution)/shard_map/all_to_all | solution.py:476
  154.5 28.4 %copy-start.15 = (f32[768,768]{1,0:T(8,128)S(1)}, f32[768,768]{1,0:T(8,128)}, u32[]{:S(2)}) copy-start(f32[768,768]{1,0:T(8,128)} %broadcast_multiply_fusion.normed_ref) | copy-start | bytes 7077892
  154.5 28.4 %copy-start.16 = (f32[256,768]{1,0:T(8,128)S(1)}, f32[256,768]{1,0:T(8,128)}, u32[]{:S(2)}) copy-start(f32[256,768]{1,0:T(8,128)} %get-tuple-element.81) | copy-start | bytes 2359300
  154.5 16.3 %collective-permute-start.3 = (bf16[256,512]{1,0:T(8,128)(2,1)}, bf16[256,512]{1,0:T(8,128)(2,1)S(1)}, u32[]{:S(2)}, u32[]{:S(2)}) collective-permute-start(bf16[256,512]{1,0:T(8,128)(2,1)} %get-tuple-element.83), channel_id=1, source_target_pairs={{1,0},{2,1},{3,2},{5,4},{6,5},{7,6},{9,8},{10,9},{11,10},{13,12},{... | collective-permute-start | bytes 786440 | tf_op jit(solution)/shard_map/ppermute | solution.py:471
  158.3 24.6 %collective-permute-start.4 = (bf16[256,512]{1,0:T(8,128)(2,1)}, bf16[256,512]{1,0:T(8,128)(2,1)S(1)}, u32[]{:S(2)}, u32[]{:S(2)}) collective-permute-start(bf16[256,512]{1,0:T(8,128)(2,1)} %get-tuple-element.84), channel_id=1, source_target_pairs={{2,0},{3,1},{6,4},{7,5},{10,8},{11,9},{14,12},{15,13},{18,16},{19,... | collective-permute-start | bytes 786440 | tf_op jit(solution)/shard_map/ppermute | solution.py:474
  187.4 23.9 %all-to-all-start.1 = ((bf16[16,40,896]{2,1,0:T(8,128)(2,1)}), bf16[16,40,896]{2,1,0:T(8,128)(2,1)}, u32[]{:S(2)}, u32[]{:S(2)}) async-start(bf16[16,40,896]{2,1,0:T(8,128)(2,1)} %bitcast.50), calls=%async_computation.2 | async-start | bytes 2293760 | tf_op jit(solution)/shard_map/all_to_all | solution.py:486
  197.9 5.3 %collective-permute-start.6 = (bf16[160,256]{1,0:T(8,128)(2,1)S(1)}, bf16[160,256]{1,0:T(8,128)(2,1)S(1)}, u32[]{:S(2)}, u32[]{:S(2)}) collective-permute-start(bf16[160,256]{1,0:T(8,128)(2,1)S(1)} %reduce_sum.52), channel_id=1, source_target_pairs={{0,2},{1,3},{2,0},{3,1},{4,6},{5,7},{6,4},{7,5},{8,10},{9,11},{10,... | collective-permute-start | bytes 245768 | tf_op jit(solution)/shard_map/ppermute | solution.py:480
  198.0 6.1 %collective-permute-start.7 = (bf16[160,256]{1,0:T(8,128)(2,1)S(1)}, bf16[160,256]{1,0:T(8,128)(2,1)S(1)}, u32[]{:S(2)}, u32[]{:S(2)}) collective-permute-start(bf16[160,256]{1,0:T(8,128)(2,1)S(1)} %reduce_sum.52), channel_id=1, source_target_pairs={{0,1},{1,2},{2,3},{3,0},{4,5},{5,6},{6,7},{7,4},{8,9},{9,10},{10,1... | collective-permute-start | bytes 245768 | tf_op jit(solution)/shard_map/ppermute | solution.py:480
  198.9 5.9 %collective-permute-start.8 = (bf16[160,256]{1,0:T(8,128)(2,1)S(1)}, bf16[160,256]{1,0:T(8,128)(2,1)S(1)}, u32[]{:S(2)}, u32[]{:S(2)}) collective-permute-start(bf16[160,256]{1,0:T(8,128)(2,1)S(1)} %reduce_sum.52), channel_id=1, source_target_pairs={{0,3},{1,0},{2,1},{3,2},{4,7},{5,4},{6,5},{7,6},{8,11},{9,8},{10,9... | collective-permute-start | bytes 245768 | tf_op jit(solution)/shard_map/ppermute | solution.py:480
  202.4 13.2 %copy-start.17 = (f32[256,768]{1,0:T(8,128)S(1)}, f32[256,768]{1,0:T(8,128)}, u32[]{:S(2)}) copy-start(f32[256,768]{1,0:T(8,128)} %multiply_add_fusion) | copy-start | bytes 2359300
  212.8 6.3 %copy-start.1 = (bf16[256,640]{1,0:T(8,128)(2,1)S(1)}, bf16[256,640]{1,0:T(8,128)(2,1)}, u32[]{:S(2)}) copy-start(bf16[256,640]{1,0:T(8,128)(2,1)} %param.17) | copy-start | bytes 983044
  212.8 4.3 %collective-permute-start.9 = (f32[20,1664]{1,0:T(8,128)S(1)}, f32[20,1664]{1,0:T(8,128)S(1)}, u32[]{:S(2)}, u32[]{:S(2)}) collective-permute-start(f32[20,1664]{1,0:T(8,128)S(1)} %constant_dynamic-slice_fusion), channel_id=1, source_target_pairs={{0,4},{4,0},{1,5},{5,1},{2,6},{6,2},{3,7},{7,3},{8,12},{12,8},{9,1... | collective-permute-start | bytes 399368 | tf_op jit(solution)/shard_map/ppermute | solution.py:501
Sparse Core Ops, SparseCore 0:
  11.8 78.6 all-gather.2
  128.2 59.1 reduce-scatter.1

commit v2 on v1

--- a/solution.py
+++ b/solution.py
@@ -435,7 +435,7 @@
         word=core_word,
         weights=(gathered, ATT, FFC),
         flops=10**10,
-        vmem=46,
+        vmem=50,
     )
     swap = [(0, 1), (1, 0)]
     arrived_ff = lax.ppermute(away_ff, "core", swap)

time: 227 us -> 224 us (0.987)
  waiting for transfers between devices: 89.6 us -> 87.3 us
where the time goes in v2:
time: 224 us; the launch traced here: 223 us
  waiting for transfers between devices  87.3 us (39%)
  Pallas kernels  42.4 us (19%)
  starting transfers between devices  28.8 us (13%)
  other arithmetic  26.8 us (12%)
  local copies, waits for them, and re-layouts  14.5 us (6%)
  between operations  14.5 us (6%)
  matrix products  9.06 us (4%)
    all_gather x1, waiting for transfers between devices, per_device(): lax.all_gather(packed, EVERY, axis=0, tiled=False)  47.5 us
    pallas_call x4, Pallas kernels, call(): pl.pallas_call(kernel, out_shape=[jax.ShapeDtypeStruct(shape, kind) for s...  40.7 us
    ppermute x1, waiting for transfers between devices, per_device(): lax.ppermute(grad_kv_two, 'x', [(i + 2, i) for i in range(XS - 2)])  12 us
    dot_general x5, matrix products, dot(): lax.dot_general(lhs, rhs, (((lhs_dim,), (rhs_dim,)), ((), ())), preferred...  9.06 us
    ppermute x1, waiting for transfers between devices, per_device(): lax.ppermute(grad_kv_one, 'x', [(i + 1, i) for i in range(XS - 1)])  8.85 us
    all_to_all x1, starting transfers between devices, per_device(): lax.all_to_all(column_ff.reshape(16, 40, 896), ('z', 'y'), 0, 0, tiled=True)  6.75 us
    all_to_all x1, waiting for transfers between devices, per_device(): lax.all_to_all(column_ff.reshape(16, 40, 896), ('z', 'y'), 0, 0, tiled=True)  6.43 us
    unnamed x42, local copies, waits for them, and re-layouts  6.27 us
  transfers between devices with their start and end apart: 14, of which 11 were waited for; matrix products, arithmetic and copies ran while one was open for 16% of the time, Pallas kernels for 7%

profile of v2, /device:TPU:3, one launch (start us, length us, event | category | flops | bytes accessed | tf_op | source)
XLA Modules:
  0.0 223.2 jit_solution(5703475663498259426)
XLA Ops:
  7.2 1.4 pad_maximum_fusion.1.wqo_ref
  8.6 1.4 convert_add_fusion.gains_ref
  10.0 1.7 shard_map.271
  11.7 3.8 %collective-permute-start = (bf16[256,640]{1,0:T(8,128)(2,1)}, bf16[256,640]{1,0:T(8,128)(2,1)S(1)}, u32[]{:S(2)}, u32[]{:S(2)}) collective-permute-start(bf16[256,640]{1,0:T(8,128)(2,1)} %param.16), channel_id=1, source_target_pairs={{0,2},{1,3},{4,6},{5,7},{8,10},{9,11},{12,14},{13,15},{16,18},{17,... | collective-permute-start | bytes 983048 | tf_op jit(solution)/shard_map/ppermute | solution.py:373
  15.5 1.9 collective-permute-start.1
  18.3 1.3 fusion.36
  19.6 1.3 fusion.37
  21.1 1.1 fusion.15.heads_ref
  22.2 1.4 multiply_sine_fusion
  23.6 1.4 fusion.19.bias_ref
  25.0 1.3 fusion.46.spread_ref
  26.3 1.4 fusion.22.heads_ref
  27.7 1.5 convolution_bitcast_fusion.up_ref
  29.2 2.8 %collective-permute-done.1 = bf16[256,640]{1,0:T(8,128)(2,1)S(1)} collective-permute-done((bf16[256,640]{1,0:T(8,128)(2,1)}, bf16[256,640]{1,0:T(8,128)(2,1)S(1)}, u32[]{:S(2)}, u32[]{:S(2)}) %collective-permute-start.1) | collective-permute-done | bytes 327712 | tf_op jit(solution)/shard_map/ppermute | solution.py:372
  32.0 2.6 %multiply_reduce_fusion = (f32[768]{0:T(1024)S(1)}, f32[768,768]{0,1:T(8,128)}) fusion(s32[768]{0:T(1024)S(1)} %get-tuple-element.151, s32[768]{0:T(1024)S(1)} %get-tuple-element.154, s32[768]{0:T(1024)S(1)} %get-tuple-element.152, s32[768]{0:T(1024)S(1)} %get-tuple-element.153, pred[768]{0:T(1024)(128)(4,1)S(1)} %get-tuple-element.155, ...), kind=kOutput, calls=%fused_computation.4 | convolution fusion | flops 762543360 | bytes 3359232 | tf_op jit(solution)/shard_map/dot_general | solution.py:54
  34.6 3.1 %copy.36 = f32[768,768]{1,0:T(8,128)} copy(f32[768,768]{0,1:T(8,128)} %get-tuple-element.136) | data formatting | bytes 4718592 | tf_op jit(solution)/shard_map/dot_general | solution.py:54
  37.6 2.1 slice.29.resid_ref
  39.7 3.3 %broadcast_multiply_fusion.normed_ref = f32[768,768]{1,0:T(8,128)} fusion(f32[768,768]{1,0:T(8,128)} %copy.36, f32[768]{0:T(1024)S(1)} %add_rsqrt_fusion), kind=kLoop, calls=%fused_computation.12 | loop fusion | flops 589824 | bytes 4721664 | tf_op jit(solution)/shard_map/mul | solution.py:38
  43.0 47.5 %all-gather.3.cloned.1.call-done = bf16[3072,2304]{1,0:T(8,128)(2,1)} async-done(((bf16[24,2304]{1,0:T(8,128)(2,1)}), bf16[3072,2304]{1,0:T(8,128)(2,1)}) %all-gather.3.cloned.1.call-update) | async-done | bytes 14155792 | tf_op jit(solution)/shard_map/all_gather | solution.py:370
  90.6 23.6 %shard_map.272 = (f32[16,768]{1,0:T(8,128)S(1)}, f32[256,1024]{1,0:T(8,128)}, f32[768,256]{1,0:T(8,128)}, bf16[256,1024]{1,0:T(8,128)(2,1)S(1)}, bf16[768,256]{1...) custom-call(s32[1]{0:T(128)} %bitcast.core_ref, ...), custom_call_target="tpu_custom_call" | custom-call | flops 10000000000 | bytes 20971520 | tf_op jit(solution)/shard_map/pallas_call | solution.py:321
  114.5 1.4 copy-done.4
  116.0 1.2 copy-done.5
  117.2 1.2 copy-done.6
  118.4 1.0 copy-done.8
  119.5 1.5 shard_map.273
  121.1 1.1 collective-permute-done.2
  122.2 3.2 %add_convert_fusion = bf16[4,640,896]{2,1,0:T(8,128)(2,1)} fusion(bf16[4,640,896]{2,1,0:T(8,128)(2,1)S(1)} %collective-permute-done.2, bf16[4,640,896]{2,1,0:T(8,128)(2,1)S(1)} %shard_map.273), kind=kLoop, calls=%fused_computation | loop fusion | flops 9175040 | bytes 13762560 | tf_op jit(solution)/shard_map/convert_element_type | solution.py:445
  125.5 14.9 %shard_map.274 = (bf16[16,4,40,256]{3,2,1,0:T(8,128)(2,1)}, bf16[16,4,40,256]{3,2,1,0:T(8,128)(2,1)}, bf16[256,512]{1,0:T(8,128)(2,1)}, bf16[256,512]{1,0:T(8,12...) custom-call(s32[1]{0:T(128)} %bitcast.core_ref, bf16[32,4,24,2304]{3,2,1,0:T(8,128)(2,1)} %bitcast.47, ...), custom_call_target="tpu_custom_call" | custom-call | flops 4000000000 | bytes 20971520 | tf_op jit(solution)/shard_map/pallas_call | solution.py:321
  140.7 3.0 %collective-permute-done.5 = bf16[16,4,40,256]{3,2,1,0:T(8,128)(2,1)S(1)} collective-permute-done((bf16[16,4,40,256]{3,2,1,0:T(8,128)(2,1)}, bf16[16,4,40,256]{3,2,1,0:T(8,128)(2,1)S(1)}, u32[]{:S(2)}, u32[]{:S(2)}) %collective-permute-start.5) | collective-permute-done | bytes 1310752 | tf_op jit(solution)/shard_map/ppermute | solution.py:470
  143.7 2.9 %add_convert_fusion.1 = bf16[16,4,40,256]{3,2,1,0:T(8,128)(2,1)} fusion(bf16[16,4,40,256]{3,2,1,0:T(8,128)(2,1)S(1)} %collective-permute-done.5, bf16[16,4,40,256]{3,2,1,0:T(8,128)(2,1)} %get-tuple-element.85), kind=kLoop, calls=%fused_computation.3 | loop fusion | flops 2621440 | bytes 3932160 | tf_op jit(solution)/shard_map/convert_element_type | solution.py:475
  146.6 5.1 %all-to-all-start = ((bf16[16,160,256]{2,1,0:T(8,128)(2,1)}), bf16[16,160,256]{2,1,0:T(8,128)(2,1)}, u32[]{:S(2)}, u32[]{:S(2)}) async-start(bf16[16,160,256]{2,1,0:T(8,128)(2,1)} %bitcast.13), calls=%async_computation | async-start | bytes 2621440 | tf_op jit(solution)/shard_map/all_to_all | solution.py:476
  151.8 3.7 %collective-permute-start.3 = (bf16[256,512]{1,0:T(8,128)(2,1)S(1)}, bf16[256,512]{1,0:T(8,128)(2,1)S(1)}, u32[]{:S(2)}, u32[]{:S(2)}) collective-permute-start(bf16[256,512]{1,0:T(8,128)(2,1)S(1)} %copy-done.19), channel_id=1, source_target_pairs={{1,0},{2,1},{3,2},{5,4},{6,5},{7,6},{9,8},{10,9},{11,10},{13,12},{... | collective-permute-start | bytes 786440 | tf_op jit(solution)/shard_map/ppermute | solution.py:471
  155.5 1.3 collective-permute-start.4
  156.8 1.2 slice_bitcast_fusion
  159.1 8.9 %collective-permute-done.3 = bf16[256,512]{1,0:T(8,128)(2,1)S(1)} collective-permute-done((bf16[256,512]{1,0:T(8,128)(2,1)S(1)}, bf16[256,512]{1,0:T(8,128)(2,1)S(1)}, u32[]{:S(2)}, u32[]{:S(2)}) %collective-permute-start.3) | collective-permute-done | bytes 262176 | tf_op jit(solution)/shard_map/ppermute | solution.py:471
  167.9 12.0 %collective-permute-done.4 = bf16[256,512]{1,0:T(8,128)(2,1)S(1)} collective-permute-done((bf16[256,512]{1,0:T(8,128)(2,1)S(1)}, bf16[256,512]{1,0:T(8,128)(2,1)S(1)}, u32[]{:S(2)}, u32[]{:S(2)}) %collective-permute-start.4) | collective-permute-done | bytes 262176 | tf_op jit(solution)/shard_map/ppermute | solution.py:474
  180.0 1.6 multiply_reduce_fusion.1
  181.6 3.1 %reduce-scatter.2.cloned.1.call-done = bf16[640,896]{1,0:T(8,128)(2,1)} async-done(((bf16[2560,896]{1,0:T(8,128)(2,1)}), bf16[640,896]{1,0:T(8,128)(2,1)}) %reduce-scatter.2.cloned.1.call-update) | async-done | bytes 1146896 | tf_op jit(solution)/shard_map/reduce_scatter | solution.py:447
  184.7 6.8 %all-to-all-start.1 = ((bf16[16,40,896]{2,1,0:T(8,128)(2,1)}), bf16[16,40,896]{2,1,0:T(8,128)(2,1)}, u32[]{:S(2)}, u32[]{:S(2)}) async-start(bf16[16,40,896]{2,1,0:T(8,128)(2,1)} %bitcast.50), calls=%async_computation.2 | async-start | bytes 2293760 | tf_op jit(solution)/shard_map/all_to_all | solution.py:486
  191.5 2.2 %multiply_add_fusion = f32[256,768]{1,0:T(8,128)} fusion(f32[256,768]{1,0:T(8,128)} %get-tuple-element.61, f32[256,768]{1,0:T(8,128)S(1)} %get-tuple-element.138, f32[768,768]{1,0:T(8,128)S(1)} %copy-done.14, f32[256]{0:T(256)S(1)} %broadcast_multiply_fusion.1, f32[256]{0:T(256)S(1)} %slice.24), kind=kLoop, calls=%fused_computation.23 | loop fusion | flops 786432 | bytes 3147776 | tf_op jit(solution)/shard_map/add | solution.py:496
  193.7 1.5 reduce_sum.52
  195.3 1.0 collective-permute-start.7
  196.3 1.7 collective-permute-start.8
  198.0 1.8 fusion.24
  202.3 6.4 %all-to-all-done.1 = bf16[16,40,896]{2,1,0:T(8,128)(2,1)} async-done(((bf16[16,40,896]{2,1,0:T(8,128)(2,1)}), bf16[16,40,896]{2,1,0:T(8,128)(2,1)}, u32[]{:S(2)}, u32[]{:S(2)}) %all-to-all-start.1) | async-done | bytes 1146912 | tf_op jit(solution)/shard_map/all_to_all | solution.py:486
  208.7 1.4 convert_reduce_fusion
  210.2 2.7 %collective-permute-start.9 = (f32[20,1664]{1,0:T(8,128)S(1)}, f32[20,1664]{1,0:T(8,128)S(1)}, u32[]{:S(2)}, u32[]{:S(2)}) collective-permute-start(f32[20,1664]{1,0:T(8,128)S(1)} %constant_dynamic-slice_fusion), channel_id=1, source_target_pairs={{0,4},{4,0},{1,5},{5,1},{2,6},{6,2},{3,7},{7,3},{8,12},{12,8},{9,1... | collective-permute-start | bytes 399368 | tf_op jit(solution)/shard_map/ppermute | solution.py:501
  212.9 1.5 convolution_add_fusion.1
  (77 shorter events, 7.4 us)
Async XLA Ops:
  7.2 20.5 %copy-start = (bf16[256,640]{1,0:T(8,128)(2,1)S(1)}, bf16[256,640]{1,0:T(8,128)(2,1)}, u32[]{:S(2)}) copy-start(bf16[256,640]{1,0:T(8,128)(2,1)} %param.17) | copy-start | bytes 983044
  7.2 83.4 %all-gather.3.cloned.1.call-start = ((), (), s32[]{:S(2)}) async-start(), calls=%async_computation.4 | async-start | bytes 14266368 | tf_op jit(solution)/shard_map/all_gather | solution.py:370
  11.7 173.1 %reduce-scatter.2.cloned.1.call-start = ((), (), s32[]{:S(2)}) async-start(), calls=%async_computation.3 | async-start | bytes 5734400 | tf_op jit(solution)/shard_map/reduce_scatter | solution.py:447
  11.7 17.5 %collective-permute-start = (bf16[256,640]{1,0:T(8,128)(2,1)}, bf16[256,640]{1,0:T(8,128)(2,1)S(1)}, u32[]{:S(2)}, u32[]{:S(2)}) collective-permute-start(bf16[256,640]{1,0:T(8,128)(2,1)} %param.16), channel_id=1, source_target_pairs={{0,2},{1,3},{4,6},{5,7},{8,10},{9,11},{12,14},{13,15},{16,18},{17,... | collective-permute-start | bytes 983048 | tf_op jit(solution)/shard_map/ppermute | solution.py:373
  15.5 16.4 %collective-permute-start.1 = (bf16[256,640]{1,0:T(8,128)(2,1)}, bf16[256,640]{1,0:T(8,128)(2,1)S(1)}, u32[]{:S(2)}, u32[]{:S(2)}) collective-permute-start(bf16[256,640]{1,0:T(8,128)(2,1)} %param.16), channel_id=1, source_target_pairs={{0,1},{1,2},{2,3},{4,5},{5,6},{6,7},{8,9},{9,10},{10,11},{12,13},{... | collective-permute-start | bytes 983048 | tf_op jit(solution)/shard_map/ppermute | solution.py:372
  23.6 66.9 %copy-start.2 = (f32[768,128]{1,0:T(8,128)}, f32[768,128]{1,0:T(8,128)S(1)}, u32[]{:S(2)}) copy-start(f32[768,128]{1,0:T(8,128)S(1)} %get-tuple-element.133.sine_ref) | copy-start | bytes 1179652
  23.6 66.9 %copy-start.3 = (f32[768,128]{1,0:T(8,128)}, f32[768,128]{1,0:T(8,128)S(1)}, u32[]{:S(2)}) copy-start(f32[768,128]{1,0:T(8,128)S(1)} %get-tuple-element.134.cosine_ref) | copy-start | bytes 1179652
  27.7 4.3 %copy-start.17 = (bf16[256,640]{1,0:T(8,128)(2,1)S(1)}, bf16[256,640]{1,0:T(8,128)(2,1)}, u32[]{:S(2)}) copy-start(bf16[256,640]{1,0:T(8,128)(2,1)} %param.16) | copy-start | bytes 983044
  114.1 6.9 %copy-start.7 = (bf16[256,1024]{1,0:T(8,128)(2,1)}, bf16[256,1024]{1,0:T(8,128)(2,1)S(1)}, u32[]{:S(2)}) copy-start(bf16[256,1024]{1,0:T(8,128)(2,1)S(1)} %get-tuple-element.74.q_ref) | copy-start | bytes 1572868
  114.2 6.9 %copy-start.9 = (bf16[768,256]{1,0:T(8,128)(2,1)}, bf16[768,256]{1,0:T(8,128)(2,1)S(1)}, u32[]{:S(2)}) copy-start(bf16[768,256]{1,0:T(8,128)(2,1)S(1)} %get-tuple-element.75.k_ref) | copy-start | bytes 1179652
  114.2 6.9 %copy-start.10 = (bf16[768,256]{1,0:T(8,128)(2,1)}, bf16[768,256]{1,0:T(8,128)(2,1)S(1)}, u32[]{:S(2)}) copy-start(bf16[768,256]{1,0:T(8,128)(2,1)S(1)} %get-tuple-element.76.v_ref) | copy-start | bytes 1179652
  114.2 6.9 %copy-start.11 = (bf16[256,768]{1,0:T(8,128)(2,1)}, bf16[256,768]{1,0:T(8,128)(2,1)S(1)}, u32[]{:S(2)}) copy-start(bf16[256,768]{1,0:T(8,128)(2,1)S(1)} %get-tuple-element.71.dattn_ref) | copy-start | bytes 1179652
  114.2 6.9 %copy-start.12 = (f32[16,768]{1,0:T(8,128)}, f32[16,768]{1,0:T(8,128)S(1)}, u32[]{:S(2)}) copy-start(f32[16,768]{1,0:T(8,128)S(1)} %get-tuple-element.78.gains_ref) | copy-start | bytes 147460
  114.2 6.9 %copy-start.13 = (f32[8,768]{1,0:T(8,128)}, f32[8,768]{1,0:T(8,128)S(1)}, u32[]{:S(2)}) copy-start(f32[8,768]{1,0:T(8,128)S(1)} %get-tuple-element.79.sums_ref) | copy-start | bytes 73732
  114.2 8.0 %collective-permute-start.2 = (bf16[4,640,896]{2,1,0:T(8,128)(2,1)}, bf16[4,640,896]{2,1,0:T(8,128)(2,1)S(1)}, u32[]{:S(2)}, u32[]{:S(2)}) collective-permute-start(bf16[4,640,896]{2,1,0:T(8,128)(2,1)} %get-tuple-element.69), channel_id=1, source_target_pairs={{0,4},{4,0},{1,5},{5,1},{2,6},{6,2},{3,7},{7,3},{8,12},{12,8},{9,1... | collective-permute-start | bytes 13762568 | tf_op jit(solution)/shard_map/ppermute | solution.py:441
  114.5 1.4 copy-start.4
  116.0 1.2 copy-start.5
  117.2 1.2 copy-start.6
  118.4 1.0 copy-start.8
  140.4 3.3 %collective-permute-start.5 = (bf16[16,4,40,256]{3,2,1,0:T(8,128)(2,1)}, bf16[16,4,40,256]{3,2,1,0:T(8,128)(2,1)S(1)}, u32[]{:S(2)}, u32[]{:S(2)}) collective-permute-start(bf16[16,4,40,256]{3,2,1,0:T(8,128)(2,1)} %get-tuple-element.86), channel_id=1, source_target_pairs={{0,4},{4,0},{1,5},{5,1},{2,6},{6,2},{3,7},{7,3},{8,12},{12,8},{9,1... | collective-permute-start | bytes 3932168 | tf_op jit(solution)/shard_map/ppermute | solution.py:470
  146.6 5.2 %copy-start.19 = (bf16[256,512]{1,0:T(8,128)(2,1)S(1)}, bf16[256,512]{1,0:T(8,128)(2,1)}, u32[]{:S(2)}) copy-start(bf16[256,512]{1,0:T(8,128)(2,1)} %get-tuple-element.83) | copy-start | bytes 786436
  146.6 8.9 %copy-start.18 = (bf16[256,512]{1,0:T(8,128)(2,1)S(1)}, bf16[256,512]{1,0:T(8,128)(2,1)}, u32[]{:S(2)}) copy-start(bf16[256,512]{1,0:T(8,128)(2,1)} %get-tuple-element.84) | copy-start | bytes 786436
  146.6 35.0 %all-to-all-start = ((bf16[16,160,256]{2,1,0:T(8,128)(2,1)}), bf16[16,160,256]{2,1,0:T(8,128)(2,1)}, u32[]{:S(2)}, u32[]{:S(2)}) async-start(bf16[16,160,256]{2,1,0:T(8,128)(2,1)} %bitcast.13), calls=%async_computation | async-start | bytes 2621440 | tf_op jit(solution)/shard_map/all_to_all | solution.py:476
  151.8 28.2 %copy-start.14 = (f32[768,768]{1,0:T(8,128)S(1)}, f32[768,768]{1,0:T(8,128)}, u32[]{:S(2)}) copy-start(f32[768,768]{1,0:T(8,128)} %broadcast_multiply_fusion.normed_ref) | copy-start | bytes 7077892
  151.8 28.2 %copy-start.16 = (bf16[256,512]{1,0:T(8,128)(2,1)S(1)}, bf16[256,512]{1,0:T(8,128)(2,1)}, u32[]{:S(2)}) copy-start(bf16[256,512]{1,0:T(8,128)(2,1)} %get-tuple-element.82) | copy-start | bytes 786436
  151.8 16.1 %collective-permute-start.3 = (bf16[256,512]{1,0:T(8,128)(2,1)S(1)}, bf16[256,512]{1,0:T(8,128)(2,1)S(1)}, u32[]{:S(2)}, u32[]{:S(2)}) collective-permute-start(bf16[256,512]{1,0:T(8,128)(2,1)S(1)} %copy-done.19), channel_id=1, source_target_pairs={{1,0},{2,1},{3,2},{5,4},{6,5},{7,6},{9,8},{10,9},{11,10},{13,12},{... | collective-permute-start | bytes 786440 | tf_op jit(solution)/shard_map/ppermute | solution.py:471
  155.5 24.5 %collective-permute-start.4 = (bf16[256,512]{1,0:T(8,128)(2,1)S(1)}, bf16[256,512]{1,0:T(8,128)(2,1)S(1)}, u32[]{:S(2)}, u32[]{:S(2)}) collective-permute-start(bf16[256,512]{1,0:T(8,128)(2,1)S(1)} %copy-done.18), channel_id=1, source_target_pairs={{2,0},{3,1},{6,4},{7,5},{10,8},{11,9},{14,12},{15,13},{18,16},{19,... | collective-permute-start | bytes 786440 | tf_op jit(solution)/shard_map/ppermute | solution.py:474
  184.7 23.9 %all-to-all-start.1 = ((bf16[16,40,896]{2,1,0:T(8,128)(2,1)}), bf16[16,40,896]{2,1,0:T(8,128)(2,1)}, u32[]{:S(2)}, u32[]{:S(2)}) async-start(bf16[16,40,896]{2,1,0:T(8,128)(2,1)} %bitcast.50), calls=%async_computation.2 | async-start | bytes 2293760 | tf_op jit(solution)/shard_map/all_to_all | solution.py:486
  195.2 5.3 %collective-permute-start.6 = (bf16[160,256]{1,0:T(8,128)(2,1)S(1)}, bf16[160,256]{1,0:T(8,128)(2,1)S(1)}, u32[]{:S(2)}, u32[]{:S(2)}) collective-permute-start(bf16[160,256]{1,0:T(8,128)(2,1)S(1)} %reduce_sum.52), channel_id=1, source_target_pairs={{0,2},{1,3},{2,0},{3,1},{4,6},{5,7},{6,4},{7,5},{8,10},{9,11},{10,... | collective-permute-start | bytes 245768 | tf_op jit(solution)/shard_map/ppermute | solution.py:480
  195.3 6.1 %collective-permute-start.7 = (bf16[160,256]{1,0:T(8,128)(2,1)S(1)}, bf16[160,256]{1,0:T(8,128)(2,1)S(1)}, u32[]{:S(2)}, u32[]{:S(2)}) collective-permute-start(bf16[160,256]{1,0:T(8,128)(2,1)S(1)} %reduce_sum.52), channel_id=1, source_target_pairs={{0,1},{1,2},{2,3},{3,0},{4,5},{5,6},{6,7},{7,4},{8,9},{9,10},{10,1... | collective-permute-start | bytes 245768 | tf_op jit(solution)/shard_map/ppermute | solution.py:480
  196.3 5.9 %collective-permute-start.8 = (bf16[160,256]{1,0:T(8,128)(2,1)S(1)}, bf16[160,256]{1,0:T(8,128)(2,1)S(1)}, u32[]{:S(2)}, u32[]{:S(2)}) collective-permute-start(bf16[160,256]{1,0:T(8,128)(2,1)S(1)} %reduce_sum.52), channel_id=1, source_target_pairs={{0,3},{1,0},{2,1},{3,2},{4,7},{5,4},{6,5},{7,6},{8,11},{9,8},{10,9... | collective-permute-start | bytes 245768 | tf_op jit(solution)/shard_map/ppermute | solution.py:480
  199.8 13.2 %copy-start.15 = (f32[256,768]{1,0:T(8,128)S(1)}, f32[256,768]{1,0:T(8,128)}, u32[]{:S(2)}) copy-start(f32[256,768]{1,0:T(8,128)} %multiply_add_fusion) | copy-start | bytes 2359300
  210.1 6.3 %copy-start.1 = (bf16[256,640]{1,0:T(8,128)(2,1)S(1)}, bf16[256,640]{1,0:T(8,128)(2,1)}, u32[]{:S(2)}) copy-start(bf16[256,640]{1,0:T(8,128)(2,1)} %param.17) | copy-start | bytes 983044
  210.2 4.3 %collective-permute-start.9 = (f32[20,1664]{1,0:T(8,128)S(1)}, f32[20,1664]{1,0:T(8,128)S(1)}, u32[]{:S(2)}, u32[]{:S(2)}) collective-permute-start(f32[20,1664]{1,0:T(8,128)S(1)} %constant_dynamic-slice_fusion), channel_id=1, source_target_pairs={{0,4},{4,0},{1,5},{5,1},{2,6},{6,2},{3,7},{7,3},{8,12},{12,8},{9,1... | collective-permute-start | bytes 399368 | tf_op jit(solution)/shard_map/ppermute | solution.py:501
Sparse Core Ops, SparseCore 0:
  11.8 78.6 all-gather.2
  125.6 59.1 reduce-scatter.1

commit v3 on v2

--- a/solution.py
+++ b/solution.py
@@ -95,7 +95,7 @@
     )
     kv = jnp.where(jnp.broadcast_to(at % 2, (OWN, 128)) == 0, kv[:, :128], kv[:, 128:])
     out[0:OWN, 512:640] = kv.astype(BF)
-    out[:, 640:768] = gains_ref[...].T[:PAD].astype(BF)
+    out[:, 640:648] = gains_ref[...].T[:PAD].astype(BF)
     out[0:OWN, 768:1280] = wg_ref[...]
     out[0:OWN, 1280:1792] = wu_ref[...]
     out[0:OWN, 1792:2304] = wd_ref[...]
@@ -350,13 +350,13 @@
     at = lax.axis_index("x")
     core = lax.axis_index("core")
 
-    gains_own = jnp.zeros((128, 128), F32)
+    gains_own = jnp.zeros((8, 128), F32)
     for row, gain in enumerate(
         (gain_input, gain_attn, gain_ffin, gain_ffout, gain_query, gain_key)
     ):
         size = gain.shape[0]
         gains_own = gains_own + jnp.pad(
-            gain.astype(F32)[None], ((row, 127 - row), (0, 128 - size))
+            gain.astype(F32)[None], ((row, 7 - row), (0, 128 - size))
         )
     width = ATT + FFC
     at_word = at.astype(jnp.int32).reshape(1)

time: 224 us -> 224 us (level)
  no operation moved by 1% of the time
where the time goes in v3:
time: 224 us; the launch traced here: 223 us
  waiting for transfers between devices  87.2 us (39%)
  Pallas kernels  42.2 us (19%)
  starting transfers between devices  28.8 us (13%)
  other arithmetic  26.7 us (12%)
  local copies, waits for them, and re-layouts  14.5 us (6%)
  between operations  14.5 us (6%)
  matrix products  9.07 us (4%)
    all_gather x1, waiting for transfers between devices, per_device(): lax.all_gather(packed, EVERY, axis=0, tiled=False)  47.5 us
    pallas_call x4, Pallas kernels, call(): pl.pallas_call(kernel, out_shape=[jax.ShapeDtypeStruct(shape, kind) for s...  40.7 us
    ppermute x1, waiting for transfers between devices, per_device(): lax.ppermute(grad_kv_two, 'x', [(i + 2, i) for i in range(XS - 2)])  12 us
    dot_general x5, matrix products, dot(): lax.dot_general(lhs, rhs, (((lhs_dim,), (rhs_dim,)), ((), ())), preferred...  9.07 us
    ppermute x1, waiting for transfers between devices, per_device(): lax.ppermute(grad_kv_one, 'x', [(i + 1, i) for i in range(XS - 1)])  8.88 us
    all_to_all x1, starting transfers between devices, per_device(): lax.all_to_all(column_ff.reshape(16, 40, 896), ('z', 'y'), 0, 0, tiled=True)  6.77 us
    all_to_all x1, waiting for transfers between devices, per_device(): lax.all_to_all(column_ff.reshape(16, 40, 896), ('z', 'y'), 0, 0, tiled=True)  6.42 us
    unnamed x42, local copies, waits for them, and re-layouts  6.27 us
  transfers between devices with their start and end apart: 14, of which 11 were waited for; matrix products, arithmetic and copies ran while one was open for 16% of the time, Pallas kernels for 7%

profile of v3, /device:TPU:3, one launch (start us, length us, event | category | flops | bytes accessed | tf_op | source)
XLA Modules:
  0.0 223.1 jit_solution(924105459665075158)
XLA Ops:
  7.2 1.4 pad_maximum_fusion.1.wqo_ref
  8.6 1.3 convert_add_fusion.gains_ref
  10.0 1.5 shard_map.271
  11.6 3.8 %collective-permute-start = (bf16[256,640]{1,0:T(8,128)(2,1)}, bf16[256,640]{1,0:T(8,128)(2,1)S(1)}, u32[]{:S(2)}, u32[]{:S(2)}) collective-permute-start(bf16[256,640]{1,0:T(8,128)(2,1)} %param.16), channel_id=1, source_target_pairs={{0,2},{1,3},{4,6},{5,7},{8,10},{9,11},{12,14},{13,15},{16,18},{17,... | collective-permute-start | bytes 983048 | tf_op jit(solution)/shard_map/ppermute | solution.py:373
  15.3 1.9 collective-permute-start.1
  18.1 1.3 fusion.36
  19.5 1.3 fusion.37
  20.9 1.1 fusion.15.heads_ref
  22.0 1.4 multiply_sine_fusion
  23.5 1.4 fusion.19.bias_ref
  24.8 1.3 fusion.46.spread_ref
  26.1 1.4 fusion.22.heads_ref
  27.5 1.5 convolution_bitcast_fusion.up_ref
  29.0 2.8 %collective-permute-done.1 = bf16[256,640]{1,0:T(8,128)(2,1)S(1)} collective-permute-done((bf16[256,640]{1,0:T(8,128)(2,1)}, bf16[256,640]{1,0:T(8,128)(2,1)S(1)}, u32[]{:S(2)}, u32[]{:S(2)}) %collective-permute-start.1) | collective-permute-done | bytes 327712 | tf_op jit(solution)/shard_map/ppermute | solution.py:372
  31.8 2.6 %multiply_reduce_fusion = (f32[768]{0:T(1024)S(1)}, f32[768,768]{0,1:T(8,128)}) fusion(s32[768]{0:T(1024)S(1)} %get-tuple-element.151, s32[768]{0:T(1024)S(1)} %get-tuple-element.154, s32[768]{0:T(1024)S(1)} %get-tuple-element.152, s32[768]{0:T(1024)S(1)} %get-tuple-element.153, pred[768]{0:T(1024)(128)(4,1)S(1)} %get-tuple-element.155, ...), kind=kOutput, calls=%fused_computation.4 | convolution fusion | flops 762543360 | bytes 3359232 | tf_op jit(solution)/shard_map/dot_general | solution.py:54
  34.4 3.1 %copy.36 = f32[768,768]{1,0:T(8,128)} copy(f32[768,768]{0,1:T(8,128)} %get-tuple-element.136) | data formatting | bytes 4718592 | tf_op jit(solution)/shard_map/dot_general | solution.py:54
  37.5 2.1 slice.29.resid_ref
  39.6 3.3 %broadcast_multiply_fusion.normed_ref = f32[768,768]{1,0:T(8,128)} fusion(f32[768,768]{1,0:T(8,128)} %copy.36, f32[768]{0:T(1024)S(1)} %add_rsqrt_fusion), kind=kLoop, calls=%fused_computation.12 | loop fusion | flops 589824 | bytes 4721664 | tf_op jit(solution)/shard_map/mul | solution.py:38
  42.8 47.5 %all-gather.3.cloned.1.call-done = bf16[3072,2304]{1,0:T(8,128)(2,1)} async-done(((bf16[24,2304]{1,0:T(8,128)(2,1)}), bf16[3072,2304]{1,0:T(8,128)(2,1)}) %all-gather.3.cloned.1.call-update) | async-done | bytes 14155792 | tf_op jit(solution)/shard_map/all_gather | solution.py:370
  90.4 23.6 %shard_map.272 = (f32[16,768]{1,0:T(8,128)S(1)}, f32[256,1024]{1,0:T(8,128)}, f32[768,256]{1,0:T(8,128)}, bf16[256,1024]{1,0:T(8,128)(2,1)S(1)}, bf16[768,256]{1...) custom-call(s32[1]{0:T(128)} %bitcast.core_ref, ...), custom_call_target="tpu_custom_call" | custom-call | flops 10000000000 | bytes 20971520 | tf_op jit(solution)/shard_map/pallas_call | solution.py:321
  114.4 1.4 copy-done.4
  115.8 1.2 copy-done.5
  117.0 1.2 copy-done.6
  118.2 1.0 copy-done.8
  119.3 1.5 shard_map.273
  120.9 1.1 collective-permute-done.2
  122.0 3.2 %add_convert_fusion = bf16[4,640,896]{2,1,0:T(8,128)(2,1)} fusion(bf16[4,640,896]{2,1,0:T(8,128)(2,1)S(1)} %collective-permute-done.2, bf16[4,640,896]{2,1,0:T(8,128)(2,1)S(1)} %shard_map.273), kind=kLoop, calls=%fused_computation | loop fusion | flops 9175040 | bytes 13762560 | tf_op jit(solution)/shard_map/convert_element_type | solution.py:445
  125.3 14.9 %shard_map.274 = (bf16[16,4,40,256]{3,2,1,0:T(8,128)(2,1)}, bf16[16,4,40,256]{3,2,1,0:T(8,128)(2,1)}, bf16[256,512]{1,0:T(8,128)(2,1)}, bf16[256,512]{1,0:T(8,12...) custom-call(s32[1]{0:T(128)} %bitcast.core_ref, bf16[32,4,24,2304]{3,2,1,0:T(8,128)(2,1)} %bitcast.47, ...), custom_call_target="tpu_custom_call" | custom-call | flops 4000000000 | bytes 20971520 | tf_op jit(solution)/shard_map/pallas_call | solution.py:321
  140.5 3.0 %collective-permute-done.5 = bf16[16,4,40,256]{3,2,1,0:T(8,128)(2,1)S(1)} collective-permute-done((bf16[16,4,40,256]{3,2,1,0:T(8,128)(2,1)}, bf16[16,4,40,256]{3,2,1,0:T(8,128)(2,1)S(1)}, u32[]{:S(2)}, u32[]{:S(2)}) %collective-permute-start.5) | collective-permute-done | bytes 1310752 | tf_op jit(solution)/shard_map/ppermute | solution.py:470
  143.5 2.9 %add_convert_fusion.1 = bf16[16,4,40,256]{3,2,1,0:T(8,128)(2,1)} fusion(bf16[16,4,40,256]{3,2,1,0:T(8,128)(2,1)S(1)} %collective-permute-done.5, bf16[16,4,40,256]{3,2,1,0:T(8,128)(2,1)} %get-tuple-element.85), kind=kLoop, calls=%fused_computation.3 | loop fusion | flops 2621440 | bytes 3932160 | tf_op jit(solution)/shard_map/convert_element_type | solution.py:475
  146.4 5.2 %all-to-all-start = ((bf16[16,160,256]{2,1,0:T(8,128)(2,1)}), bf16[16,160,256]{2,1,0:T(8,128)(2,1)}, u32[]{:S(2)}, u32[]{:S(2)}) async-start(bf16[16,160,256]{2,1,0:T(8,128)(2,1)} %bitcast.13), calls=%async_computation | async-start | bytes 2621440 | tf_op jit(solution)/shard_map/all_to_all | solution.py:476
  151.7 3.6 %collective-permute-start.3 = (bf16[256,512]{1,0:T(8,128)(2,1)S(1)}, bf16[256,512]{1,0:T(8,128)(2,1)S(1)}, u32[]{:S(2)}, u32[]{:S(2)}) collective-permute-start(bf16[256,512]{1,0:T(8,128)(2,1)S(1)} %copy-done.19), channel_id=1, source_target_pairs={{1,0},{2,1},{3,2},{5,4},{6,5},{7,6},{9,8},{10,9},{11,10},{13,12},{... | collective-permute-start | bytes 786440 | tf_op jit(solution)/shard_map/ppermute | solution.py:471
  155.3 1.3 collective-permute-start.4
  156.6 1.2 slice_bitcast_fusion
  158.9 8.9 %collective-permute-done.3 = bf16[256,512]{1,0:T(8,128)(2,1)S(1)} collective-permute-done((bf16[256,512]{1,0:T(8,128)(2,1)S(1)}, bf16[256,512]{1,0:T(8,128)(2,1)S(1)}, u32[]{:S(2)}, u32[]{:S(2)}) %collective-permute-start.3) | collective-permute-done | bytes 262176 | tf_op jit(solution)/shard_map/ppermute | solution.py:471
  167.8 12.0 %collective-permute-done.4 = bf16[256,512]{1,0:T(8,128)(2,1)S(1)} collective-permute-done((bf16[256,512]{1,0:T(8,128)(2,1)S(1)}, bf16[256,512]{1,0:T(8,128)(2,1)S(1)}, u32[]{:S(2)}, u32[]{:S(2)}) %collective-permute-start.4) | collective-permute-done | bytes 262176 | tf_op jit(solution)/shard_map/ppermute | solution.py:474
  179.8 1.6 multiply_reduce_fusion.1
  181.5 3.1 %reduce-scatter.2.cloned.1.call-done = bf16[640,896]{1,0:T(8,128)(2,1)} async-done(((bf16[2560,896]{1,0:T(8,128)(2,1)}), bf16[640,896]{1,0:T(8,128)(2,1)}) %reduce-scatter.2.cloned.1.call-update) | async-done | bytes 1146896 | tf_op jit(solution)/shard_map/reduce_scatter | solution.py:447
  184.6 6.8 %all-to-all-start.1 = ((bf16[16,40,896]{2,1,0:T(8,128)(2,1)}), bf16[16,40,896]{2,1,0:T(8,128)(2,1)}, u32[]{:S(2)}, u32[]{:S(2)}) async-start(bf16[16,40,896]{2,1,0:T(8,128)(2,1)} %bitcast.50), calls=%async_computation.2 | async-start | bytes 2293760 | tf_op jit(solution)/shard_map/all_to_all | solution.py:486
  191.3 2.2 %multiply_add_fusion = f32[256,768]{1,0:T(8,128)} fusion(f32[256,768]{1,0:T(8,128)} %get-tuple-element.61, f32[256,768]{1,0:T(8,128)S(1)} %get-tuple-element.138, f32[768,768]{1,0:T(8,128)S(1)} %copy-done.14, f32[256]{0:T(256)S(1)} %broadcast_multiply_fusion.1, f32[256]{0:T(256)S(1)} %slice.24), kind=kLoop, calls=%fused_computation.23 | loop fusion | flops 786432 | bytes 3147776 | tf_op jit(solution)/shard_map/add | solution.py:496
  193.6 1.5 reduce_sum.52
  195.2 1.0 collective-permute-start.7
  196.1 1.7 collective-permute-start.8
  197.8 1.8 fusion.24
  202.1 6.4 %all-to-all-done.1 = bf16[16,40,896]{2,1,0:T(8,128)(2,1)} async-done(((bf16[16,40,896]{2,1,0:T(8,128)(2,1)}), bf16[16,40,896]{2,1,0:T(8,128)(2,1)}, u32[]{:S(2)}, u32[]{:S(2)}) %all-to-all-start.1) | async-done | bytes 1146912 | tf_op jit(solution)/shard_map/all_to_all | solution.py:486
  208.5 1.4 convert_reduce_fusion
  210.0 2.8 %collective-permute-start.9 = (f32[20,1664]{1,0:T(8,128)S(1)}, f32[20,1664]{1,0:T(8,128)S(1)}, u32[]{:S(2)}, u32[]{:S(2)}) collective-permute-start(f32[20,1664]{1,0:T(8,128)S(1)} %constant_dynamic-slice_fusion), channel_id=1, source_target_pairs={{0,4},{4,0},{1,5},{5,1},{2,6},{6,2},{3,7},{7,3},{8,12},{12,8},{9,1... | collective-permute-start | bytes 399368 | tf_op jit(solution)/shard_map/ppermute | solution.py:501
  212.8 1.5 convolution_add_fusion.1
  (77 shorter events, 7.4 us)
Async XLA Ops:
  7.2 20.3 %copy-start = (bf16[256,640]{1,0:T(8,128)(2,1)S(1)}, bf16[256,640]{1,0:T(8,128)(2,1)}, u32[]{:S(2)}) copy-start(bf16[256,640]{1,0:T(8,128)(2,1)} %param.17) | copy-start | bytes 983044
  7.2 83.2 %all-gather.3.cloned.1.call-start = ((), (), s32[]{:S(2)}) async-start(), calls=%async_computation.4 | async-start | bytes 14266368 | tf_op jit(solution)/shard_map/all_gather | solution.py:370
  11.5 173.0 %reduce-scatter.2.cloned.1.call-start = ((), (), s32[]{:S(2)}) async-start(), calls=%async_computation.3 | async-start | bytes 5734400 | tf_op jit(solution)/shard_map/reduce_scatter | solution.py:447
  11.6 17.5 %collective-permute-start = (bf16[256,640]{1,0:T(8,128)(2,1)}, bf16[256,640]{1,0:T(8,128)(2,1)S(1)}, u32[]{:S(2)}, u32[]{:S(2)}) collective-permute-start(bf16[256,640]{1,0:T(8,128)(2,1)} %param.16), channel_id=1, source_target_pairs={{0,2},{1,3},{4,6},{5,7},{8,10},{9,11},{12,14},{13,15},{16,18},{17,... | collective-permute-start | bytes 983048 | tf_op jit(solution)/shard_map/ppermute | solution.py:373
  15.3 16.4 %collective-permute-start.1 = (bf16[256,640]{1,0:T(8,128)(2,1)}, bf16[256,640]{1,0:T(8,128)(2,1)S(1)}, u32[]{:S(2)}, u32[]{:S(2)}) collective-permute-start(bf16[256,640]{1,0:T(8,128)(2,1)} %param.16), channel_id=1, source_target_pairs={{0,1},{1,2},{2,3},{4,5},{5,6},{6,7},{8,9},{9,10},{10,11},{12,13},{... | collective-permute-start | bytes 983048 | tf_op jit(solution)/shard_map/ppermute | solution.py:372
  23.4 66.9 %copy-start.2 = (f32[768,128]{1,0:T(8,128)}, f32[768,128]{1,0:T(8,128)S(1)}, u32[]{:S(2)}) copy-start(f32[768,128]{1,0:T(8,128)S(1)} %get-tuple-element.133.sine_ref) | copy-start | bytes 1179652
  23.5 66.9 %copy-start.3 = (f32[768,128]{1,0:T(8,128)}, f32[768,128]{1,0:T(8,128)S(1)}, u32[]{:S(2)}) copy-start(f32[768,128]{1,0:T(8,128)S(1)} %get-tuple-element.134.cosine_ref) | copy-start | bytes 1179652
  27.5 4.3 %copy-start.17 = (bf16[256,640]{1,0:T(8,128)(2,1)S(1)}, bf16[256,640]{1,0:T(8,128)(2,1)}, u32[]{:S(2)}) copy-start(bf16[256,640]{1,0:T(8,128)(2,1)} %param.16) | copy-start | bytes 983044
  113.9 6.9 %copy-start.7 = (bf16[256,1024]{1,0:T(8,128)(2,1)}, bf16[256,1024]{1,0:T(8,128)(2,1)S(1)}, u32[]{:S(2)}) copy-start(bf16[256,1024]{1,0:T(8,128)(2,1)S(1)} %get-tuple-element.74.q_ref) | copy-start | bytes 1572868
  114.0 6.9 %copy-start.9 = (bf16[768,256]{1,0:T(8,128)(2,1)}, bf16[768,256]{1,0:T(8,128)(2,1)S(1)}, u32[]{:S(2)}) copy-start(bf16[768,256]{1,0:T(8,128)(2,1)S(1)} %get-tuple-element.75.k_ref) | copy-start | bytes 1179652
  114.0 6.9 %copy-start.10 = (bf16[768,256]{1,0:T(8,128)(2,1)}, bf16[768,256]{1,0:T(8,128)(2,1)S(1)}, u32[]{:S(2)}) copy-start(bf16[768,256]{1,0:T(8,128)(2,1)S(1)} %get-tuple-element.76.v_ref) | copy-start | bytes 1179652
  114.0 6.9 %copy-start.11 = (bf16[256,768]{1,0:T(8,128)(2,1)}, bf16[256,768]{1,0:T(8,128)(2,1)S(1)}, u32[]{:S(2)}) copy-start(bf16[256,768]{1,0:T(8,128)(2,1)S(1)} %get-tuple-element.71.dattn_ref) | copy-start | bytes 1179652
  114.0 6.9 %copy-start.12 = (f32[16,768]{1,0:T(8,128)}, f32[16,768]{1,0:T(8,128)S(1)}, u32[]{:S(2)}) copy-start(f32[16,768]{1,0:T(8,128)S(1)} %get-tuple-element.78.gains_ref) | copy-start | bytes 147460
  114.0 6.9 %copy-start.13 = (f32[8,768]{1,0:T(8,128)}, f32[8,768]{1,0:T(8,128)S(1)}, u32[]{:S(2)}) copy-start(f32[8,768]{1,0:T(8,128)S(1)} %get-tuple-element.79.sums_ref) | copy-start | bytes 73732
  114.0 8.0 %collective-permute-start.2 = (bf16[4,640,896]{2,1,0:T(8,128)(2,1)}, bf16[4,640,896]{2,1,0:T(8,128)(2,1)S(1)}, u32[]{:S(2)}, u32[]{:S(2)}) collective-permute-start(bf16[4,640,896]{2,1,0:T(8,128)(2,1)} %get-tuple-element.69), channel_id=1, source_target_pairs={{0,4},{4,0},{1,5},{5,1},{2,6},{6,2},{3,7},{7,3},{8,12},{12,8},{9,1... | collective-permute-start | bytes 13762568 | tf_op jit(solution)/shard_map/ppermute | solution.py:441
  114.4 1.4 copy-start.4
  115.8 1.2 copy-start.5
  117.0 1.2 copy-start.6
  118.2 1.0 copy-start.8
  140.2 3.3 %collective-permute-start.5 = (bf16[16,4,40,256]{3,2,1,0:T(8,128)(2,1)}, bf16[16,4,40,256]{3,2,1,0:T(8,128)(2,1)S(1)}, u32[]{:S(2)}, u32[]{:S(2)}) collective-permute-start(bf16[16,4,40,256]{3,2,1,0:T(8,128)(2,1)} %get-tuple-element.86), channel_id=1, source_target_pairs={{0,4},{4,0},{1,5},{5,1},{2,6},{6,2},{3,7},{7,3},{8,12},{12,8},{9,1... | collective-permute-start | bytes 3932168 | tf_op jit(solution)/shard_map/ppermute | solution.py:470
  146.4 5.2 %copy-start.19 = (bf16[256,512]{1,0:T(8,128)(2,1)S(1)}, bf16[256,512]{1,0:T(8,128)(2,1)}, u32[]{:S(2)}) copy-start(bf16[256,512]{1,0:T(8,128)(2,1)} %get-tuple-element.83) | copy-start | bytes 786436
  146.4 8.9 %copy-start.18 = (bf16[256,512]{1,0:T(8,128)(2,1)S(1)}, bf16[256,512]{1,0:T(8,128)(2,1)}, u32[]{:S(2)}) copy-start(bf16[256,512]{1,0:T(8,128)(2,1)} %get-tuple-element.84) | copy-start | bytes 786436
  146.4 35.0 %all-to-all-start = ((bf16[16,160,256]{2,1,0:T(8,128)(2,1)}), bf16[16,160,256]{2,1,0:T(8,128)(2,1)}, u32[]{:S(2)}, u32[]{:S(2)}) async-start(bf16[16,160,256]{2,1,0:T(8,128)(2,1)} %bitcast.13), calls=%async_computation | async-start | bytes 2621440 | tf_op jit(solution)/shard_map/all_to_all | solution.py:476
  151.6 28.2 %copy-start.14 = (f32[768,768]{1,0:T(8,128)S(1)}, f32[768,768]{1,0:T(8,128)}, u32[]{:S(2)}) copy-start(f32[768,768]{1,0:T(8,128)} %broadcast_multiply_fusion.normed_ref) | copy-start | bytes 7077892
  151.6 28.2 %copy-start.16 = (bf16[256,512]{1,0:T(8,128)(2,1)S(1)}, bf16[256,512]{1,0:T(8,128)(2,1)}, u32[]{:S(2)}) copy-start(bf16[256,512]{1,0:T(8,128)(2,1)} %get-tuple-element.82) | copy-start | bytes 786436
  151.7 16.1 %collective-permute-start.3 = (bf16[256,512]{1,0:T(8,128)(2,1)S(1)}, bf16[256,512]{1,0:T(8,128)(2,1)S(1)}, u32[]{:S(2)}, u32[]{:S(2)}) collective-permute-start(bf16[256,512]{1,0:T(8,128)(2,1)S(1)} %copy-done.19), channel_id=1, source_target_pairs={{1,0},{2,1},{3,2},{5,4},{6,5},{7,6},{9,8},{10,9},{11,10},{13,12},{... | collective-permute-start | bytes 786440 | tf_op jit(solution)/shard_map/ppermute | solution.py:471
  155.3 24.5 %collective-permute-start.4 = (bf16[256,512]{1,0:T(8,128)(2,1)S(1)}, bf16[256,512]{1,0:T(8,128)(2,1)S(1)}, u32[]{:S(2)}, u32[]{:S(2)}) collective-permute-start(bf16[256,512]{1,0:T(8,128)(2,1)S(1)} %copy-done.18), channel_id=1, source_target_pairs={{2,0},{3,1},{6,4},{7,5},{10,8},{11,9},{14,12},{15,13},{18,16},{19,... | collective-permute-start | bytes 786440 | tf_op jit(solution)/shard_map/ppermute | solution.py:474
  184.6 23.9 %all-to-all-start.1 = ((bf16[16,40,896]{2,1,0:T(8,128)(2,1)}), bf16[16,40,896]{2,1,0:T(8,128)(2,1)}, u32[]{:S(2)}, u32[]{:S(2)}) async-start(bf16[16,40,896]{2,1,0:T(8,128)(2,1)} %bitcast.50), calls=%async_computation.2 | async-start | bytes 2293760 | tf_op jit(solution)/shard_map/all_to_all | solution.py:486
  195.1 5.3 %collective-permute-start.6 = (bf16[160,256]{1,0:T(8,128)(2,1)S(1)}, bf16[160,256]{1,0:T(8,128)(2,1)S(1)}, u32[]{:S(2)}, u32[]{:S(2)}) collective-permute-start(bf16[160,256]{1,0:T(8,128)(2,1)S(1)} %reduce_sum.52), channel_id=1, source_target_pairs={{0,2},{1,3},{2,0},{3,1},{4,6},{5,7},{6,4},{7,5},{8,10},{9,11},{10,... | collective-permute-start | bytes 245768 | tf_op jit(solution)/shard_map/ppermute | solution.py:480
  195.2 6.1 %collective-permute-start.7 = (bf16[160,256]{1,0:T(8,128)(2,1)S(1)}, bf16[160,256]{1,0:T(8,128)(2,1)S(1)}, u32[]{:S(2)}, u32[]{:S(2)}) collective-permute-start(bf16[160,256]{1,0:T(8,128)(2,1)S(1)} %reduce_sum.52), channel_id=1, source_target_pairs={{0,1},{1,2},{2,3},{3,0},{4,5},{5,6},{6,7},{7,4},{8,9},{9,10},{10,1... | collective-permute-start | bytes 245768 | tf_op jit(solution)/shard_map/ppermute | solution.py:480
  196.1 5.9 %collective-permute-start.8 = (bf16[160,256]{1,0:T(8,128)(2,1)S(1)}, bf16[160,256]{1,0:T(8,128)(2,1)S(1)}, u32[]{:S(2)}, u32[]{:S(2)}) collective-permute-start(bf16[160,256]{1,0:T(8,128)(2,1)S(1)} %reduce_sum.52), channel_id=1, source_target_pairs={{0,3},{1,0},{2,1},{3,2},{4,7},{5,4},{6,5},{7,6},{8,11},{9,8},{10,9... | collective-permute-start | bytes 245768 | tf_op jit(solution)/shard_map/ppermute | solution.py:480
  199.6 13.2 %copy-start.15 = (f32[256,768]{1,0:T(8,128)S(1)}, f32[256,768]{1,0:T(8,128)}, u32[]{:S(2)}) copy-start(f32[256,768]{1,0:T(8,128)} %multiply_add_fusion) | copy-start | bytes 2359300
  210.0 6.3 %copy-start.1 = (bf16[256,640]{1,0:T(8,128)(2,1)S(1)}, bf16[256,640]{1,0:T(8,128)(2,1)}, u32[]{:S(2)}) copy-start(bf16[256,640]{1,0:T(8,128)(2,1)} %param.17) | copy-start | bytes 983044
  210.0 4.3 %collective-permute-start.9 = (f32[20,1664]{1,0:T(8,128)S(1)}, f32[20,1664]{1,0:T(8,128)S(1)}, u32[]{:S(2)}, u32[]{:S(2)}) collective-permute-start(f32[20,1664]{1,0:T(8,128)S(1)} %constant_dynamic-slice_fusion), channel_id=1, source_target_pairs={{0,4},{4,0},{1,5},{5,1},{2,6},{6,2},{3,7},{7,3},{8,12},{12,8},{9,1... | collective-permute-start | bytes 399368 | tf_op jit(solution)/shard_map/ppermute | solution.py:501
Sparse Core Ops, SparseCore 0:
  11.6 78.6 all-gather.2
  125.4 59.1 reduce-scatter.1
